TPU v7x, 128 devices: a whole 4x4x4 slice. The times are simulated.
128 devices in a mesh: seq: 32 (over x, z, core), head: 4 (over y).
Axes of the slice: x: 4, y: 4, z: 4, core: 2. Of those that a mesh axis runs over, the one named last changes fastest.
Arguments:
- queries: bfloat16 [32768, 1024], P(('seq', 'head')), may hold values from -8 to 8
- keys: bfloat16 [32768, 1024], P(('seq', 'head')), may hold values from -8 to 8
- values: bfloat16 [32768, 1024], P(('seq', 'head')), may hold values from -6 to 6
- out_grad: bfloat16 [32768, 1024], P(('seq', 'head')), may hold values from -6 to 6
- random_blocks: int32 [256, 3], replicated, may hold values from 0 to 255, as said below
- global_blocks: int32 [2], replicated, may hold values from 0 to 255, as said below
Outputs:
- grad_queries: bfloat16 [32768, 1024], P(('seq', 'head'))
- grad_keys: bfloat16 [32768, 1024], P(('seq', 'head'))
- grad_values: bfloat16 [32768, 1024], P(('seq', 'head'))
Inputs may be any that keep to these rules, and one draw needn't show every extreme that they name: `random_blocks`: row i lists the random key blocks of query block i; repeats may occur. Among the 24 entries of the rows of one index of seq (rows b with the same b // 8), at most 2 name blocks of any one index of seq; in every draw some index of seq is named exactly 2 times from every index. `global_blocks`: 2 different block numbers in any order; one of them is always the last block, 255.
All inputs are finite; a program needn't handle non-finite values.
Results may differ from a plain program's by a relative error of at most 0.006.
Values may be sent and summed in bfloat16 or wider, within the bound.
No kernel may reach another device: no remote copies, remote signals or barrier semaphores. Data moves between devices by JAX's collectives and lax.ppermute only.
A program may use at most 192 MiB of HBM per device.

v0:
```python
import math

import jax
import jax.numpy as jnp
from jax import lax
from jax.sharding import PartitionSpec as P

HEAD_DIM = 128
BLOCK = 128


masked_score = -1e30


def padded_2(block, sides, width):
    for axis, dim in sides:
        count = lax.axis_size(axis)
        forward = [(i, i + 1) for i in range(count - 1)]
        backward = [(target, source) for source, target in forward]
        low = lax.ppermute(
            lax.slice_in_dim(block, block.shape[dim] - width, None, axis=dim), axis, forward
        )
        high = lax.ppermute(lax.slice_in_dim(block, 0, width, axis=dim), axis, backward)
        block = jnp.concatenate([low, block, high], axis=dim)
    return block


def from_behind(block, axis, distance):
    devices = range(lax.axis_size(axis))
    route = [(i - distance, i) for i in devices if i - distance in devices]
    return lax.ppermute(block, axis, route)


def rounded(tensor):
    return lax.optimization_barrier(tensor.astype(jnp.bfloat16)).astype(jnp.float32)


def split_pairs(keyset, head_count, head_size):
    groups, slot_num, block_len, pair_width = keyset.shape
    pieces = keyset.reshape(groups, slot_num * block_len, 2, head_count, head_size)
    return (pieces[:, :, 0], pieces[:, :, 1])


def score_rows(queries, keyset, present, block_len, score_scale):
    scores = (
        jnp.einsum("gthd,gkhd->ghtk", queries, keyset, preferred_element_type=jnp.float32)
        * score_scale
    )
    key_mask = jnp.repeat(present, block_len, axis=1)[:, None, None, :]
    return jnp.where(key_mask, scores, masked_score)


def value_rows(out_grads, valset):
    return jnp.einsum("gthd,gkhd->ghtk", out_grads, valset, preferred_element_type=jnp.float32)


def grad_terms(row_probs, prob_grad, row_delta, queries, out_grads, keyset, block_len, score_scale):
    probs_low = row_probs.astype(jnp.bfloat16)
    dscore = (row_probs * (prob_grad - row_delta) * score_scale).astype(jnp.bfloat16)
    groups, head_count, row_num, total_keys = dscore.shape
    slot_num = total_keys // block_len
    head_size = keyset.shape[-1]
    row_width = head_count * head_size
    dq_slots = jnp.einsum(
        "ghtsk,gskhd->gsthd",
        dscore.reshape(groups, head_count, row_num, slot_num, block_len),
        keyset.reshape(groups, slot_num, block_len, head_count, head_size),
        preferred_element_type=jnp.float32,
    )
    key_grad = jnp.einsum("ghtk,gthd->gkhd", dscore, queries, preferred_element_type=jnp.float32)
    value_grad = jnp.einsum(
        "ghtk,gthd->gkhd", probs_low, out_grads, preferred_element_type=jnp.float32
    )
    pair_terms = jnp.concatenate(
        [
            key_grad.reshape(groups, slot_num, block_len, row_width),
            value_grad.reshape(groups, slot_num, block_len, row_width),
        ],
        axis=-1,
    )
    return (dq_slots.reshape(groups, slot_num, row_num, row_width), pair_terms)


def add_window(window_sum, pair_terms, row_start, group_size):
    for offset in range(3):
        segment = (
            lax.dynamic_slice_in_dim(window_sum, row_start + offset, group_size, 0)
            + pair_terms[:, offset]
        )
        window_sum = lax.dynamic_update_slice_in_dim(window_sum, segment, row_start + offset, 0)
    return window_sum


def fold_owned(pair_terms, owned_ids, block_count):
    onehot = (owned_ids[:, None] == jnp.arange(block_count)[None, :]).astype(jnp.bfloat16)
    flattened = pair_terms.reshape(pair_terms.shape[0], -1)
    summed = jnp.einsum("sb,sk->bk", onehot, flattened, preferred_element_type=jnp.float32)
    return summed.reshape((block_count,) + pair_terms.shape[1:])


def local(queries, keys, values, out_grad, random_blocks, global_blocks):
    query_rows, key_rows, value_rows_in, grad_rows = (
        lax.all_to_all(queries, "head", split_axis=1, concat_axis=0, tiled=True),
        lax.all_to_all(keys, "head", split_axis=1, concat_axis=0, tiled=True),
        lax.all_to_all(values, "head", split_axis=1, concat_axis=0, tiled=True),
        lax.all_to_all(out_grad, "head", split_axis=1, concat_axis=0, tiled=True),
    )
    block_len = BLOCK
    head_size = HEAD_DIM
    token_count, row_width = query_rows.shape
    head_count = row_width // head_size
    block_count = token_count // block_len
    seq_devices = lax.axis_size("seq")
    seq_position = lax.axis_index("seq")
    all_blocks = block_count * seq_devices
    score_scale = 1.0 / math.sqrt(head_size)
    glob_count = global_blocks.shape[0]
    rand_count = random_blocks.shape[1]
    local_slots = 3 + glob_count
    request_count = block_count * rand_count
    capacity = (request_count + seq_devices - 1) // seq_devices + 1
    slot_total = seq_devices * capacity
    group_size = math.gcd(block_count, 4)
    group_count = block_count // group_size
    first_block = seq_position * block_count
    query_blocks = query_rows.reshape(block_count, block_len, head_count, head_size)
    grad_blocks = grad_rows.reshape(block_count, block_len, head_count, head_size)
    pair_rows = jnp.concatenate([key_rows, value_rows_in], axis=1)
    padded = padded_2(pair_rows, (("seq", 0),), block_len).reshape(
        block_count + 2, block_len, 2 * row_width
    )
    pair_blocks = padded[1 : block_count + 1]
    glob_local = global_blocks - first_block
    glob_owned = (glob_local >= 0) & (glob_local < block_count)
    glob_pick = pair_blocks[jnp.clip(glob_local, 0, block_count - 1)]
    glob_term = jnp.where(glob_owned[:, None, None], glob_pick, jnp.zeros_like(glob_pick)).astype(
        jnp.float32
    )
    glob_pairs = lax.psum(glob_term.astype(jnp.bfloat16), "seq")
    glob_set = jnp.broadcast_to(glob_pairs[None], (group_size,) + glob_pairs.shape)
    own_lists = lax.dynamic_slice_in_dim(random_blocks, first_block, block_count, 0).reshape(
        request_count
    )
    request_owner = own_lists // block_count
    owner_hits = (request_owner[:, None] == jnp.arange(seq_devices)[None, :]).astype(jnp.int32)
    owner_rank = jnp.sum((jnp.cumsum(owner_hits, axis=0) - owner_hits) * owner_hits, axis=1)
    slot_index = request_owner * capacity + owner_rank
    every_list = random_blocks.reshape(seq_devices, request_count)
    asked_here = (every_list // block_count == seq_position).astype(jnp.int32)
    asked_rank = jnp.where(asked_here == 1, jnp.cumsum(asked_here, axis=1) - asked_here, capacity)
    senders = jnp.broadcast_to(jnp.arange(seq_devices)[:, None], (seq_devices, request_count))
    served_ids = (
        jnp.zeros((seq_devices, capacity + 1), jnp.int32)
        .at[senders, asked_rank]
        .set(every_list % block_count)[:, :capacity]
        .reshape(slot_total)
    )
    query_index = first_block + jnp.arange(block_count)
    present = jnp.concatenate(
        [
            (query_index > 0)[:, None],
            jnp.ones((block_count, 1), bool),
            (query_index < all_blocks - 1)[:, None],
            jnp.ones((block_count, glob_count + rand_count), bool),
        ],
        axis=1,
    )

    def window_set(row_start):
        near_blocks = lax.dynamic_slice_in_dim(padded, row_start, group_size + 2, 0)
        return jnp.stack(
            [
                near_blocks[0:group_size],
                near_blocks[1 : group_size + 1],
                near_blocks[2 : group_size + 2],
            ],
            axis=1,
        )

    def group_inputs(row_start):
        group_query = lax.dynamic_slice_in_dim(query_blocks, row_start, group_size, 0)
        group_grad = lax.dynamic_slice_in_dim(grad_blocks, row_start, group_size, 0)
        group_mask = lax.dynamic_slice_in_dim(present, row_start, group_size, 0)
        return (group_query, group_grad, group_mask)

    window_zero = jnp.zeros((block_count + 2, block_len, 2 * row_width), jnp.float32)
    glob_zero = jnp.zeros(glob_pairs.shape, jnp.float32)
    served_pairs = pair_blocks[served_ids].reshape(seq_devices, capacity, block_len, 2 * row_width)
    fetched = lax.all_to_all(served_pairs, "seq", split_axis=0, concat_axis=0, tiled=True).reshape(
        slot_total, block_len, 2 * row_width
    )
    rand_pairs = fetched[slot_index].reshape(block_count, rand_count, block_len, 2 * row_width)

    def full_step(carried, step_index):
        window_sum, glob_sum = carried
        row_start = step_index * group_size
        group_query, group_grad, group_mask = group_inputs(row_start)
        rand_group = lax.dynamic_slice_in_dim(rand_pairs, row_start, group_size, 0)
        keyset, valset = split_pairs(
            jnp.concatenate([window_set(row_start), glob_set, rand_group], axis=1),
            head_count,
            head_size,
        )
        scores = score_rows(group_query, keyset, group_mask, block_len, score_scale)
        prob_grad = value_rows(group_grad, valset)
        row_max = jnp.max(scores, axis=-1, keepdims=True)
        weights = jnp.exp(scores - row_max)
        row_probs = weights / jnp.sum(weights, axis=-1, keepdims=True)
        row_delta = jnp.sum(row_probs * prob_grad, axis=-1, keepdims=True)
        dq_slots, pair_terms = grad_terms(
            row_probs, prob_grad, row_delta, group_query, group_grad, keyset, block_len, score_scale
        )
        query_grad = jnp.sum(dq_slots[:, :local_slots], axis=1) + jnp.sum(
            rounded(dq_slots[:, local_slots:]), axis=1
        )
        window_sum = add_window(window_sum, pair_terms, row_start, group_size)
        glob_sum = glob_sum + jnp.sum(pair_terms[:, 3:local_slots], axis=0)
        return (
            (window_sum, glob_sum),
            (query_grad, pair_terms[:, local_slots:].astype(jnp.bfloat16)),
        )

    (window_sum, glob_sum), (dq_parts, rand_terms) = lax.scan(
        full_step, (window_zero, glob_zero), jnp.arange(group_count)
    )
    dq_total = dq_parts.reshape(block_count, block_len, row_width)
    outgoing = (
        jnp.zeros((slot_total, block_len, 2 * row_width), jnp.bfloat16)
        .at[slot_index]
        .set(rand_terms.reshape(request_count, block_len, 2 * row_width))
    )
    returned = lax.all_to_all(
        outgoing.reshape(seq_devices, capacity, block_len, 2 * row_width),
        "seq",
        split_axis=0,
        concat_axis=0,
        tiled=True,
    )
    rand_sum = fold_owned(
        returned.reshape(slot_total, block_len, 2 * row_width), served_ids, block_count
    )
    from_next = from_behind(window_sum[0], "seq", -1)
    from_prev = from_behind(window_sum[block_count + 1], "seq", 1)
    glob_total = lax.psum(glob_sum, "seq")
    owned_onehot = (glob_local[:, None] == jnp.arange(block_count)[None, :]).astype(jnp.float32)
    glob_back = jnp.einsum("gb,gtc->btc", owned_onehot, glob_total, precision=lax.Precision.HIGHEST)
    pair_grad = window_sum[1 : block_count + 1] + glob_back + rand_sum
    pair_grad = pair_grad.at[0].add(from_prev).at[block_count - 1].add(from_next)
    pair_low = pair_grad.astype(jnp.bfloat16).reshape(token_count, 2 * row_width)
    query_low = dq_total.astype(jnp.bfloat16).reshape(token_count, row_width)
    return (
        lax.all_to_all(query_low, "head", split_axis=0, concat_axis=1, tiled=True),
        lax.all_to_all(pair_low[:, :row_width], "head", split_axis=0, concat_axis=1, tiled=True),
        lax.all_to_all(pair_low[:, row_width:], "head", split_axis=0, concat_axis=1, tiled=True),
    )


def solution(mesh):
    placed = (
        P(("seq", "head"), None),
        P(("seq", "head"), None),
        P(("seq", "head"), None),
        P(("seq", "head"), None),
        P(),
        P(),
    )
    return jax.shard_map(
        local,
        mesh=mesh,
        in_specs=placed,
        out_specs=(P(("seq", "head"), None), P(("seq", "head"), None), P(("seq", "head"), None)),
        check_vma=False,
    )
```

profile of v0, /device:TPU:1, one launch (start us, length us, event | category | flops | bytes accessed | tf_op | source)
XLA Modules:
  0.0 749.0 jit_solution(15614859558388187416)
XLA Ops:
  9.1 5.0 all-to-all-start
  14.1 2.0 copy.210
  16.2 6.2 all-to-all-done
  22.4 3.5 all-to-all-start.1
  27.3 5.6 all-to-all-done.1
  32.9 3.5 all-to-all-start.2
  37.8 33.2 %scatter_fusion = s32[32,3]{0,1:T(4,128)S(1)} fusion(s32[32,3]{0,1:T(4,128)S(1)} %broadcast_in_dim.110, s32[768]{0:T(1024)S(1)} %reshape.502, s32[768]{0:T(1024)S(1)} %reshape.504), kind=kCustom, calls=%fused_computation.3 | custom fusion | bytes 15360 | tf_op jit(solution)/shard_map/scatter | solution.py:155
  72.1 4.2 all-to-all-start.4
  76.8 5.5 gather_fusion
  83.2 13.2 %all-to-all-start.3 = ((bf16[32,2,128,512]{3,2,1,0:T(8,128)(2,1)}), bf16[32,2,128,512]{3,2,1,0:T(8,128)(2,1)}, u32[]{:S(2)}, u32[]{:S(2)}) async-start(bf16[32,2,128,512]{3,2,1,0:T(8,128)(2,1)} %bitcast.181), calls=%async_computation.3 | async-start | bytes 16777216 | tf_op jit(solution)/shard_map/all_to_all | solution.py:189
  98.6 3.5 collective-permute-start
  108.0 162.2 %all-reduce.3.cloned.1.call-done = bf16[2,128,512]{2,1,0:T(8,128)(2,1)} async-done(((bf16[2,128,512]{2,1,0:T(8,128)(2,1)}), bf16[2,128,512]{2,1,0:T(8,128)(2,1)}) %all-reduce.3.cloned.1.call-update) | async-done | bytes 262160 | tf_op jit(solution)/shard_map/psum | solution.py:139
  272.0 2.2 pad_maximum_fusion
  274.2 5.9 gather_fusion.1
  281.8 220.3 %while.21 = (s32[]{:T(128)}, f32[10,128,512]{1,2,0:T(8,128)}, f32[2,128,512]{1,0,2:T(2,128)}, bf16[2,4,128,256]{2,3,1,0:T(8,128)(2,1)}, bf16[2,4,3,128,512]{4,3,...) while((s32[]{:T(128)}, f32[10,128,512]{1,2,0:T(8,128)}, ...), condition=%wide.region_12.13_spmd.clone, body=%wide.region_5.12_spmd.clone.sunk | while | flops 1368003584 | bytes 311985152 | solution.py:223
  295.6 2.1 constant_dynamic-slice_fusion.8
  302.9 2.0 copy.316
  304.9 2.0 copy.317
  306.8 2.7 constant_dynamic-slice_fusion.9
  309.5 3.0 copy.318
  312.5 18.8 %concatenate.47 = bf16[4,8,128,512]{2,1,3,0:T(8,128)(2,1)} concatenate(bf16[4,1,128,512]{2,1,3,0:T(2,128)(2,1)} %copy.315, bf16[4,1,128,512]{2,1,3,0:T(2,128)(2,1)} %copy.316, bf16[4,1,128,512]{2,1,3,0:T(2,128)(2,1)} %copy.317, bf16[4,2,128,512]{2,1,3,0:T(2,128)(2,1)S(1)} %broadcast_in_dim.164, bf16[4,3,128,512]{2,1,3,0:T(4,128)(2,1)S(1)} %copy.318), dimensions={1} | concatenate | bytes 8388608 | tf_op jit(solution)/shard_map/while/body/eval_jaxpr/concatenate | solution.py:200
  331.3 7.3 reshape.528
  340.2 2.6 copy.322
  342.8 2.4 fusion.111
  348.1 2.0 copy-done.26
  350.1 5.8 fusion.117
  355.9 13.7 %fusion.114 = f32[4,2,128,1024]{3,2,1,0:T(8,128)} fusion(bf16[4,128,2,128]{3,2,1,0:T(2,128)(2,1)S(1)} %copy-done.9, f32[4,2,128,1024]{3,2,1,0:T(8,128)} %copy-done.1, f32[4,2,128,1024]{3,2,1,0:T(8,128)} %copy-done.26, f32[4,2,128]{2,1,0:T(2,128)S(1)} %get-tuple-element.431), kind=kOutput, calls=%fused_computation.44.clone.1 | convolution fusion | flops 275777536 | bytes 12849152 | tf_op jit(solution)/shard_map/while/body/eval_jaxpr/ghtk,gthd->gkhd/dot_general | solution.py:70
  369.7 3.0 fusion.115
  381.9 2.3 fusion.119
  384.1 3.1 fusion.116
  387.3 4.1 copy.323
  399.6 2.1 constant_dynamic-slice_fusion.8
  408.9 2.0 copy.317
  410.8 2.7 constant_dynamic-slice_fusion.9
  413.5 3.0 copy.318
  416.5 18.8 %concatenate.47 = bf16[4,8,128,512]{2,1,3,0:T(8,128)(2,1)} concatenate(bf16[4,1,128,512]{2,1,3,0:T(2,128)(2,1)} %copy.315, bf16[4,1,128,512]{2,1,3,0:T(2,128)(2,1)} %copy.316, bf16[4,1,128,512]{2,1,3,0:T(2,128)(2,1)} %copy.317, bf16[4,2,128,512]{2,1,3,0:T(2,128)(2,1)S(1)} %broadcast_in_dim.164, bf16[4,3,128,512]{2,1,3,0:T(4,128)(2,1)S(1)} %copy.318), dimensions={1} | concatenate | bytes 8388608 | tf_op jit(solution)/shard_map/while/body/eval_jaxpr/concatenate | solution.py:200
  435.3 7.3 reshape.528
  444.2 2.6 copy.322
  446.8 2.4 fusion.111
  452.1 2.0 copy-done.26
  454.1 5.8 fusion.117
  459.9 13.7 %fusion.114 = f32[4,2,128,1024]{3,2,1,0:T(8,128)} fusion(bf16[4,128,2,128]{3,2,1,0:T(2,128)(2,1)S(1)} %copy-done.9, f32[4,2,128,1024]{3,2,1,0:T(8,128)} %copy-done.1, f32[4,2,128,1024]{3,2,1,0:T(8,128)} %copy-done.26, f32[4,2,128]{2,1,0:T(2,128)S(1)} %get-tuple-element.431), kind=kOutput, calls=%fused_computation.44.clone.1 | convolution fusion | flops 275777536 | bytes 12849152 | tf_op jit(solution)/shard_map/while/body/eval_jaxpr/ghtk,gthd->gkhd/dot_general | solution.py:70
  473.7 3.0 fusion.115
  485.8 2.3 fusion.119
  488.1 3.1 fusion.116
  491.3 4.1 copy.323
  502.1 4.2 broadcast_in_dim.117
  506.4 7.5 %scatter_fusion.1 = bf16[64,128,512]{2,1,0:T(8,128)(2,1)} fusion(bf16[64,128,512]{2,1,0:T(8,128)(2,1)} %broadcast_in_dim.117, s32[24]{0:T(128)S(1)} %copy-done.22, bf16[24,128,512]{2,1,0:T(8,128)(2,1)S(1)} %bitcast.189), kind=kCustom, calls=%fused_computation.4 | custom fusion | bytes 9437280 | tf_op jit(solution)/shard_map/scatter | solution.py:230
  513.9 6.2 all-to-all-start.6
  520.3 2.1 copy.238
  522.4 3.5 copy.233
  526.9 2.0 copy.231
  530.7 2.2 collective-permute-start.3
  533.0 3.3 collective-permute-start.2
  536.3 90.7 %all-to-all-done.6 = bf16[32,2,128,512]{3,2,1,0:T(8,128)(2,1)} async-done(((bf16[32,2,128,512]{3,2,1,0:T(8,128)(2,1)}), bf16[32,2,128,512]{3,2,1,0:T(8,128)(2,1)}, u32[]{:S(2)}, u32[]{:S(2)}) %all-to-all-start.6) | async-done | bytes 8388640 | tf_op jit(solution)/shard_map/all_to_all | solution.py:232
  627.0 4.0 all-to-all-start.5
  630.9 13.6 %fusion.36 = f32[8,128,512]{2,0,1:T(8,128)} fusion(s32[64]{0:T(128)S(1)} %eq.79, bf16[8,8,128,512]{3,2,1,0:T(8,128)(2,1)} %bitcast.87), kind=kOutput, calls=%fused_computation.62 | convolution fusion | flops 67109376 | bytes 10486016 | tf_op jit(solution)/shard_map/sb,sk->bk/dot_general | solution.py:97
  644.6 61.1 %all-reduce.5.cloned.1.call-done = f32[2,128,512]{2,0,1:T(2,128)} async-done(((f32[2,128,512]{2,0,1:T(2,128)}), f32[2,128,512]{2,0,1:T(2,128)}) %all-reduce.5.cloned.1.call-update) | async-done | bytes 524304 | tf_op jit(solution)/shard_map/psum | solution.py:244
  705.7 5.1 fusion.39
  711.2 2.2 scatter-add.6
  713.8 2.2 scatter-add.9
  717.4 12.4 %all_to_all.134 = bf16[4,256,256]{2,1,0:T(8,128)(2,1)S(1)} all-to-all(bf16[4,256,256]{2,1,0:T(8,128)(2,1)S(1)} %bitcast.199), channel_id=1, replica_groups=mesh['seq'=32,'head'=4] {'head'}, dimensions={0} | all-to-all | bytes 1048576 | tf_op jit(solution)/shard_map/all_to_all | solution.py:253
  729.8 3.5 all-to-all-start.8
  735.7 4.9 all-to-all-done.8
  (210 shorter events, 81.5 us)
Async XLA Ops:
  7.2 18.7 %copy-start.20 = (s32[256,3]{0,1:T(4,128)S(1)}, s32[256,3]{0,1:T(4,128)}, u32[]{:S(2)}) copy-start(s32[256,3]{0,1:T(4,128)} %param.16) | copy-start | bytes 9220
  7.2 19.1 %copy-start.16 = (bf16[256,1024]{1,0:T(8,128)(2,1)S(1)}, bf16[256,1024]{1,0:T(8,128)(2,1)}, u32[]{:S(2)}) copy-start(bf16[256,1024]{1,0:T(8,128)(2,1)} %param.14) | copy-start | bytes 1572868
  9.1 13.3 %all-to-all-start = ((bf16[256,4,256]{2,0,1:T(8,128)(2,1)}), bf16[256,4,256]{2,0,1:T(8,128)(2,1)S(1)}, u32[]{:S(2)}, u32[]{:S(2)}) async-start(bf16[256,4,256]{2,0,1:T(8,128)(2,1)} %bitcast.128), calls=%async_computation | async-start | bytes 1048576 | tf_op jit(solution)/shard_map/all_to_all | solution.py:103
  22.4 10.5 %all-to-all-start.1 = ((bf16[256,4,256]{0,2,1:T(8,128)(2,1)}), bf16[256,4,256]{0,2,1:T(8,128)(2,1)S(1)}, u32[]{:S(2)}, u32[]{:S(2)}) async-start(bf16[256,4,256]{0,2,1:T(8,128)(2,1)} %bitcast.1), calls=%async_computation.1 | async-start | bytes 1048576 | tf_op jit(solution)/shard_map/all_to_all | solution.py:104
  32.9 39.2 %all-to-all-start.2 = ((bf16[256,4,256]{0,2,1:T(8,128)(2,1)}), bf16[256,4,256]{0,2,1:T(8,128)(2,1)S(1)}, u32[]{:S(2)}, u32[]{:S(2)}) async-start(bf16[256,4,256]{0,2,1:T(8,128)(2,1)} %bitcast.4), calls=%async_computation.2 | async-start | bytes 1048576 | tf_op jit(solution)/shard_map/all_to_all | solution.py:105
  37.8 33.5 %copy-start.17 = (bf16[256,1024]{1,0:T(8,128)(2,1)S(1)}, bf16[256,1024]{1,0:T(8,128)(2,1)}, u32[]{:S(2)}) copy-start(bf16[256,1024]{1,0:T(8,128)(2,1)} %param.15) | copy-start | bytes 1572868
  71.1 5.2 copy-start.18
  72.1 11.1 %all-to-all-start.4 = ((bf16[256,4,256]{2,0,1:T(8,128)(2,1)}), bf16[256,4,256]{2,0,1:T(8,128)(2,1)S(1)}, u32[]{:S(2)}, u32[]{:S(2)}) async-start(bf16[256,4,256]{2,0,1:T(8,128)(2,1)} %bitcast.127), calls=%async_computation.4 | async-start | bytes 1048576 | tf_op jit(solution)/shard_map/all_to_all | solution.py:106
  83.2 13.9 %copy-start.25 = (s32[2]{0:T(128)S(1)}, s32[2]{0:T(128)}, u32[]{:S(2)}) copy-start(s32[2]{0:T(128)} %param.17) | copy-start | bytes 28
  83.2 191.0 %all-to-all-start.3 = ((bf16[32,2,128,512]{3,2,1,0:T(8,128)(2,1)}), bf16[32,2,128,512]{3,2,1,0:T(8,128)(2,1)}, u32[]{:S(2)}, u32[]{:S(2)}) async-start(bf16[32,2,128,512]{3,2,1,0:T(8,128)(2,1)} %bitcast.181), calls=%async_computation.3 | async-start | bytes 16777216 | tf_op jit(solution)/shard_map/all_to_all | solution.py:189
  96.4 173.8 %all-reduce.3.cloned.1.call-start = ((), (), s32[]{:S(2)}) async-start(), calls=%async_computation.9 | async-start | bytes 524288 | tf_op jit(solution)/shard_map/psum | solution.py:139
  97.1 5.1 copy-start.23
  98.6 173.4 %collective-permute-start = (bf16[128,512]{1,0:T(8,128)(2,1)}, bf16[128,512]{1,0:T(8,128)(2,1)S(1)}, u32[]{:S(2)}, u32[]{:S(2)}) collective-permute-start(bf16[128,512]{1,0:T(8,128)(2,1)} %get-tuple-element.338), channel_id=1, source_target_pairs={{0,4},{4,8},{8,12},{12,16},{16,20},{20,24},{24,28},{28,32},{32,36}... | collective-permute-start | bytes 393224 | tf_op jit(solution)/shard_map/ppermute | solution.py:20
  102.2 169.8 %collective-permute-start.1 = (bf16[128,512]{1,0:T(8,128)(2,1)}, bf16[128,512]{1,0:T(8,128)(2,1)}, u32[]{:S(2)}, u32[]{:S(2)}) collective-permute-start(bf16[128,512]{1,0:T(8,128)(2,1)} %get-tuple-element.339), channel_id=1, source_target_pairs={{4,0},{8,4},{12,8},{16,12},{20,16},{24,20},{28,24},{32,28},{36,32}... | collective-permute-start | bytes 393224 | tf_op jit(solution)/shard_map/ppermute | solution.py:23
  106.2 173.9 %copy-start.21 = (s32[24]{0:T(128)}, s32[24]{0:T(128)S(1)}, u32[]{:S(2)}) copy-start(s32[24]{0:T(128)S(1)} %fusion.71) | copy-start | bytes 292
  338.6 1.6 slice-start
  342.8 2.8 copy-start
  342.8 2.8 copy-start.9
  345.6 2.5 copy-start.1
  348.1 2.0 copy-start.26
  372.7 2.2 copy-start.7
  374.9 1.6 copy-start.5
  379.5 1.7 copy-start.10
  381.8 5.4 copy-start.11
  384.1 7.2 copy-start.2
  391.4 3.4 copy-start.8
  391.4 3.6 copy-start.6
  391.4 3.6 copy-start.13
  395.0 1.5 copy-start.3
  396.5 1.6 copy-start.14
  442.6 1.6 slice-start
  446.8 2.8 copy-start
  446.8 2.8 copy-start.9
  449.6 2.5 copy-start.1
  452.1 2.0 copy-start.26
  476.7 2.2 copy-start.7
  478.8 1.6 copy-start.5
  483.5 1.7 copy-start.10
  485.8 5.4 copy-start.11
  488.1 7.2 copy-start.2
  495.4 3.4 copy-start.8
  495.4 3.6 copy-start.6
  495.4 3.6 copy-start.13
  499.0 1.5 copy-start.3
  500.5 1.6 copy-start.14
  502.1 4.2 copy-start.15
  502.1 4.2 copy-start.22
  513.9 6.2 copy-start.19
  513.9 6.4 copy-start.4
  513.9 113.1 %all-to-all-start.6 = ((bf16[32,2,128,512]{3,2,1,0:T(8,128)(2,1)}), bf16[32,2,128,512]{3,2,1,0:T(8,128)(2,1)}, u32[]{:S(2)}, u32[]{:S(2)}) async-start(bf16[32,2,128,512]{3,2,1,0:T(8,128)(2,1)} %bitcast.179), calls=%async_computation.6 | async-start | bytes 16777216 | tf_op jit(solution)/shard_map/all_to_all | solution.py:232
  520.1 185.6 %all-reduce.5.cloned.1.call-start = ((), (), s32[]{:S(2)}) async-start(), calls=%async_computation.10 | async-start | bytes 1048576 | tf_op jit(solution)/shard_map/psum | solution.py:244
  522.4 3.5 copy-start.12
  530.7 182.7 %collective-permute-start.3 = (f32[128,512]{1,0:T(8,128)}, f32[128,512]{1,0:T(8,128)S(1)}, u32[]{:S(2)}, u32[]{:S(2)}) collective-permute-start(f32[128,512]{1,0:T(8,128)} %get-tuple-element.334), channel_id=1, source_target_pairs={{4,0},{8,4},{12,8},{16,12},{20,16},{24,20},{28,24},{32,28},{36,32}... | collective-permute-start | bytes 786440 | tf_op jit(solution)/shard_map/ppermute | solution.py:31
  533.0 177.9 %collective-permute-start.2 = (f32[128,512]{1,0:T(8,128)S(1)}, f32[128,512]{1,0:T(8,128)S(1)}, u32[]{:S(2)}, u32[]{:S(2)}) collective-permute-start(f32[128,512]{1,0:T(8,128)S(1)} %get-tuple-element.335), channel_id=1, source_target_pairs={{0,4},{4,8},{8,12},{12,16},{16,20},{20,24},{24,28},{28,32},{32,36}... | collective-permute-start | bytes 786440 | tf_op jit(solution)/shard_map/ppermute | solution.py:31
  627.0 90.4 %all-to-all-start.5 = ((bf16[4,256,256]{2,1,0:T(8,128)(2,1)}), bf16[4,256,256]{2,1,0:T(8,128)(2,1)S(1)}, u32[]{:S(2)}, u32[]{:S(2)}) async-start(bf16[4,256,256]{2,1,0:T(8,128)(2,1)} %bitcast.17), calls=%async_computation.5 | async-start | bytes 1048576 | tf_op jit(solution)/shard_map/all_to_all | solution.py:252
  630.9 74.7 %copy-start.24 = (s32[2]{0:T(128)S(1)}, s32[2]{0:T(128)}, u32[]{:S(2)}) copy-start(s32[2]{0:T(128)} %copy-done.23) | copy-start | bytes 28
  729.8 10.8 %all-to-all-start.8 = ((bf16[4,256,256]{2,1,0:T(8,128)(2,1)}), bf16[4,256,256]{2,1,0:T(8,128)(2,1)S(1)}, u32[]{:S(2)}, u32[]{:S(2)}) async-start(bf16[4,256,256]{2,1,0:T(8,128)(2,1)} %bitcast.31), calls=%async_computation.8 | async-start | bytes 1048576 | tf_op jit(solution)/shard_map/all_to_all | solution.py:254
Sparse Core Ops, SparseCore 0:
  105.6 164.5 all-reduce.2
  527.0 178.5 all-reduce.4
where the time goes:
time: 762 us; the launch traced here: 749 us
  waiting for transfers between devices  332 us (44%)
  local copies, waits for them, and re-layouts  225 us (30%)
  matrix products  61.7 us (8%)
  starting transfers between devices  54 us (7%)
  other arithmetic  35 us (5%)
  between operations  14.9 us (2%)
  loops' own time  14.2 us (2%)
  blocking collectives  12.4 us (2%)
    psum x1, waiting for transfers between devices, local(): glob_pairs = lax.psum(glob_term.astype(jnp.bfloat16), 'seq')  162 us
    all_to_all x1, waiting for transfers between devices, local(): lax.all_to_all(outgoing.reshape(seq_devices, capacity, block_len, 2 * row...  90.7 us
    psum x1, waiting for transfers between devices, local(): glob_total = lax.psum(glob_sum, 'seq')  61.1 us
    concatenate x2, local copies, waits for them, and re-layouts, full_step(): jnp.concatenate([window_set(row_start), glob_set, rand_group], axis=1)  37.6 us
    scatter x1, local copies, waits for them, and re-layouts, local(): served_ids = jnp.zeros((seq_devices, capacity + 1), jnp.int32).at[senders...  33.2 us
    dot_general x2, matrix products, grad_terms(): jnp.einsum('ghtk,gthd->gkhd', dscore, queries, preferred_element_type=jnp...  27.5 us
    while x68, local copies, waits for them, and re-layouts  24.1 us
  transfers between devices with their start and end apart: 14, of which 7 were waited for; matrix products, arithmetic and copies ran while one was open for 12% of the time, Pallas kernels for 0%

commit v1 on v0

v1 whole, which is shorter than its diff:
```python
import functools
import math

import jax
import jax.numpy as jnp
from jax import lax
from jax.experimental import pallas as pl
from jax.experimental.pallas import tpu as pltpu
from jax.sharding import PartitionSpec as P

HEAD_DIM = 128
BLOCK = 128
HEADS = 8
DEVICES = 128
OWN = 2
RANDOM = 3
GLOBAL = 2
ENTRIES = OWN * RANDOM + GLOBAL
TILE = 16
TILES = BLOCK // TILE
BLOCKS = DEVICES * OWN
AXES = ("seq", "head")
SCALE = 1.0 / math.sqrt(HEAD_DIM)
SCALE_LOG2 = SCALE * math.log2(math.e)
MASKED = -1e30
VMEM_LIMIT = 48 * 1024 * 1024


def params(**kw):
    return pltpu.CompilerParams(vmem_limit_bytes=VMEM_LIMIT, **kw)


def whole(shape):
    return pl.BlockSpec(shape, lambda *_: (0,) * len(shape))


def pack_kernel(k_ref, v_ref, tiles_ref, low_ref, high_ref):
    for part, ref in enumerate((k_ref, v_ref)):
        low_ref[pl.ds(part * BLOCK, BLOCK), :] = ref[:BLOCK, :]
        high_ref[pl.ds(part * BLOCK, BLOCK), :] = ref[BLOCK:, :]
        for head in range(HEADS):
            for block in range(OWN):
                tiles_ref[pl.ds((part * HEADS + head) * TILES, TILES), block] = ref[
                    pl.ds(block * BLOCK, BLOCK), pl.ds(head * HEAD_DIM, HEAD_DIM)
                ].reshape(TILES, TILE, HEAD_DIM)


def pack(keys, values):
    width = HEADS * HEAD_DIM
    edge = jax.ShapeDtypeStruct((2 * BLOCK, width), jnp.bfloat16)
    return pl.pallas_call(
        pack_kernel,
        out_shape=(
            jax.ShapeDtypeStruct((DEVICES, OWN, TILE, HEAD_DIM), jnp.bfloat16),
            edge,
            edge,
        ),
        compiler_params=params(),
        name="pack_tiles",
    )(keys, values)


def select_kernel(random_ref, global_ref, table_ref, out_ref):
    common = [table_ref[global_ref[which]] for which in range(GLOBAL)]

    def step(device, carry):
        for entry in range(OWN * RANDOM):
            out_ref[device, entry] = table_ref[random_ref[device * (OWN * RANDOM) + entry]]
        for which in range(GLOBAL):
            out_ref[device, OWN * RANDOM + which] = common[which]
        return carry

    lax.fori_loop(0, DEVICES, step, 0, unroll=4)


def select(random_list, global_blocks, table):
    shape = (DEVICES, ENTRIES, TILE, HEAD_DIM)
    return pl.pallas_call(
        select_kernel,
        grid_spec=pltpu.PrefetchScalarGridSpec(
            num_scalar_prefetch=2,
            grid=(1,),
            in_specs=[whole(table.shape)],
            out_specs=whole(shape),
        ),
        out_shape=jax.ShapeDtypeStruct(shape, jnp.bfloat16),
        compiler_params=params(),
        name="select_tiles",
    )(random_list, global_blocks, table)


def dot_nt(a, b):
    return lax.dot_general(a, b, (((1,), (1,)), ((), ())), preferred_element_type=jnp.float32)


def dot_nn(a, b):
    return lax.dot_general(a, b, (((1,), (0,)), ((), ())), preferred_element_type=jnp.float32)


def dot_tn(a, b):
    return lax.dot_general(a, b, (((0,), (0,)), ((), ())), preferred_element_type=jnp.float32)


def attend_kernel(
    device_ref, q_ref, d_ref, k_ref, v_ref, prev_ref, next_ref, far_ref,
    dq_ref, wk_ref, wv_ref, to_prev_ref, to_next_ref, terms_ref,
):
    device = device_ref[0]
    queries = q_ref[...]
    grads = d_ref[...]

    def entry(part, index):
        return far_ref[part, 0, :, index].reshape(BLOCK, HEAD_DIM)

    def keyset(part, own_ref):
        shared = jnp.concatenate(
            [own_ref[...], entry(part, OWN * RANDOM), entry(part, OWN * RANDOM + 1)], axis=0
        )
        private = []
        for block, edge in enumerate((prev_ref, next_ref)):
            private.append(
                jnp.concatenate(
                    [edge[pl.ds(part * BLOCK, BLOCK), :]]
                    + [entry(part, block * RANDOM + r) for r in range(RANDOM)],
                    axis=0,
                )
            )
        return shared, private

    def rows(block):
        return slice(block * BLOCK, (block + 1) * BLOCK)

    k_shared, k_private = keyset(0, k_ref)
    v_shared, v_private = keyset(1, v_ref)

    s_shared = dot_nt(k_shared, queries) * SCALE_LOG2
    s_private = (
        jnp.concatenate([dot_nt(k_private[b], queries[rows(b)]) for b in range(OWN)], axis=1)
        * SCALE_LOG2
    )
    column = lax.broadcasted_iota(jnp.int32, (1, OWN * BLOCK), 1)
    absent = ((column < BLOCK) & (device == 0)) | ((column >= BLOCK) & (device == DEVICES - 1))
    s_edge = jnp.where(absent, MASKED, s_private[:BLOCK])
    s_random = s_private[BLOCK:]
    p_shared = dot_nt(v_shared, grads)
    p_private = jnp.concatenate(
        [dot_nt(v_private[b], grads[rows(b)]) for b in range(OWN)], axis=1
    )
    row_max = jnp.maximum(
        jnp.maximum(
            jnp.max(s_shared, axis=0, keepdims=True), jnp.max(s_edge, axis=0, keepdims=True)
        ),
        jnp.max(s_random, axis=0, keepdims=True),
    )
    e_shared = jnp.exp2(s_shared - row_max)
    e_private = jnp.concatenate([jnp.exp2(s_edge - row_max), jnp.exp2(s_random - row_max)], axis=0)
    total = jnp.sum(e_shared, axis=0, keepdims=True) + jnp.sum(e_private, axis=0, keepdims=True)
    inverse = 1.0 / total
    delta = (
        jnp.sum(e_shared * p_shared, axis=0, keepdims=True)
        + jnp.sum(e_private * p_private, axis=0, keepdims=True)
    ) * inverse

    probs_shared = e_shared * inverse
    probs_private = e_private * inverse
    low_shared = probs_shared.astype(jnp.bfloat16)
    low_private = probs_private.astype(jnp.bfloat16)
    ds_shared = (probs_shared * ((p_shared - delta) * SCALE)).astype(jnp.bfloat16)
    ds_private = (probs_private * ((p_private - delta) * SCALE)).astype(jnp.bfloat16)

    dq_shared = dot_tn(k_shared, ds_shared)
    dq_private = jnp.concatenate(
        [dot_tn(k_private[b], ds_private[:, rows(b)]) for b in range(OWN)], axis=1
    )
    dq_ref[...] = (dq_shared + dq_private).T.astype(jnp.bfloat16)

    for part, weights_shared, weights_private, other, own_ref in (
        (0, ds_shared, ds_private, queries, wk_ref),
        (1, low_shared, low_private, grads, wv_ref),
    ):
        shared = dot_nn(weights_shared, other)
        own_ref[...] = shared[: OWN * BLOCK]
        for which in range(GLOBAL):
            terms_ref[part, 0, :, OWN * RANDOM + which] = (
                shared[rows(OWN + which)].astype(jnp.bfloat16).reshape(TILES, TILE, HEAD_DIM)
            )
        for block, edge in enumerate((to_prev_ref, to_next_ref)):
            private = dot_nn(weights_private[:, rows(block)], other[rows(block)]).astype(
                jnp.bfloat16
            )
            edge[pl.ds(part * BLOCK, BLOCK), :] = private[:BLOCK]
            for r in range(RANDOM):
                terms_ref[part, 0, :, block * RANDOM + r] = private[rows(1 + r)].reshape(
                    TILES, TILE, HEAD_DIM
                )


def attend(device, queries, grads, keys, values, from_prev, from_next, far):
    width = HEADS * HEAD_DIM
    rows = OWN * BLOCK
    far_shape = (2, HEADS, TILES, ENTRIES, TILE, HEAD_DIM)
    column = pl.BlockSpec((rows, HEAD_DIM), lambda h, *_: (0, h))
    far_spec = pl.BlockSpec((2, 1, TILES, ENTRIES, TILE, HEAD_DIM), lambda h, *_: (0, h, 0, 0, 0, 0))
    low = jax.ShapeDtypeStruct((rows, width), jnp.bfloat16)
    high = jax.ShapeDtypeStruct((rows, width), jnp.float32)
    return pl.pallas_call(
        attend_kernel,
        grid_spec=pltpu.PrefetchScalarGridSpec(
            num_scalar_prefetch=1,
            grid=(HEADS,),
            in_specs=[column] * 6 + [far_spec],
            out_specs=[column] * 5 + [far_spec],
        ),
        out_shape=(low, high, high, low, low, jax.ShapeDtypeStruct(far_shape, jnp.bfloat16)),
        compiler_params=params(),
        name="attend",
    )(device, queries, grads, keys, values, from_prev, from_next, far.reshape(far_shape))


def collect_kernel(random_ref, global_ref, terms_ref, out_ref, *sums):
    for sum_ref in sums:
        sum_ref[...] = jnp.zeros_like(sum_ref)

    def step(device, carry):
        for entry in range(OWN * RANDOM):
            sum_ref = sums[entry % len(sums)]
            block = random_ref[device * (OWN * RANDOM) + entry]
            sum_ref[block] = sum_ref[block] + terms_ref[device, entry].astype(jnp.float32)
        return tuple(
            carry[which] + terms_ref[device, OWN * RANDOM + which].astype(jnp.float32)
            for which in range(GLOBAL)
        )

    zero = jnp.zeros((TILE, HEAD_DIM), jnp.float32)
    totals = lax.fori_loop(0, DEVICES, step, (zero,) * GLOBAL, unroll=2)
    for which in range(GLOBAL):
        block = global_ref[which]
        sums[0][block] = sums[0][block] + totals[which]
    result = sums[0][...]
    for sum_ref in sums[1:]:
        result = result + sum_ref[...]
    out_ref[...] = result.astype(jnp.bfloat16)


def collect(random_list, global_blocks, terms):
    shape = (BLOCKS, TILE, HEAD_DIM)
    return pl.pallas_call(
        collect_kernel,
        grid_spec=pltpu.PrefetchScalarGridSpec(
            num_scalar_prefetch=2,
            grid=(1,),
            in_specs=[whole(terms.shape)],
            out_specs=whole(shape),
            scratch_shapes=[pltpu.VMEM(shape, jnp.float32)] * 3,
        ),
        out_shape=jax.ShapeDtypeStruct(shape, jnp.bfloat16),
        compiler_params=params(),
        name="collect_terms",
    )(random_list, global_blocks, terms)


def finish_kernel(wk_ref, wv_ref, prev_ref, next_ref, far_ref, dk_ref, dv_ref):
    for part, (own_ref, out_ref) in enumerate(((wk_ref, dk_ref), (wv_ref, dv_ref))):
        for block, edge in enumerate((prev_ref, next_ref)):
            rows = pl.ds(block * BLOCK, BLOCK)
            far = far_ref[part, 0, :, block].reshape(BLOCK, HEAD_DIM).astype(jnp.float32)
            near = edge[pl.ds(part * BLOCK, BLOCK), :].astype(jnp.float32)
            out_ref[rows, :] = (own_ref[rows, :] + near + far).astype(jnp.bfloat16)


def finish(wk, wv, from_prev, from_next, far):
    width = HEADS * HEAD_DIM
    rows = OWN * BLOCK
    far_shape = (2, HEADS, TILES, OWN, TILE, HEAD_DIM)
    column = pl.BlockSpec((rows, HEAD_DIM), lambda h: (0, h))
    low = jax.ShapeDtypeStruct((rows, width), jnp.bfloat16)
    return pl.pallas_call(
        finish_kernel,
        grid=(HEADS,),
        in_specs=[column] * 4
        + [pl.BlockSpec((2, 1, TILES, OWN, TILE, HEAD_DIM), lambda h: (0, h, 0, 0, 0, 0))],
        out_specs=[column] * 2,
        out_shape=(low, low),
        compiler_params=params(),
        name="finish",
    )(wk, wv, from_prev, from_next, far.reshape(far_shape))


def exchange(tiles):
    return lax.all_to_all(tiles, AXES, split_axis=0, concat_axis=0, tiled=True)


UP = [(i, i + 1) for i in range(DEVICES - 1)]
DOWN = [(i + 1, i) for i in range(DEVICES - 1)]


def local(queries, keys, values, out_grad, random_blocks, global_blocks):
    device = lax.axis_index(AXES).astype(jnp.int32).reshape(1)
    random_list = random_blocks.reshape(-1)
    tiles, low, high = pack(keys, values)
    from_prev = lax.ppermute(high, AXES, UP)
    from_next = lax.ppermute(low, AXES, DOWN)
    table = exchange(tiles).reshape(BLOCKS, TILE, HEAD_DIM)
    far = exchange(select(random_list, global_blocks, table))
    dq, wk, wv, to_prev, to_next, terms = attend(
        device, queries, out_grad, keys, values, from_prev, from_next, far
    )
    grad_from_next = lax.ppermute(to_prev, AXES, DOWN)
    grad_from_prev = lax.ppermute(to_next, AXES, UP)
    returned = exchange(terms.reshape(DEVICES, ENTRIES, TILE, HEAD_DIM))
    sums = collect(random_list, global_blocks, returned)
    back = exchange(sums.reshape(DEVICES, OWN, TILE, HEAD_DIM))
    dk, dv = finish(wk, wv, grad_from_prev, grad_from_next, back)
    return dq, dk, dv


def solution(mesh):
    split = P(AXES, None)
    return jax.shard_map(
        local,
        mesh=mesh,
        in_specs=(split, split, split, split, P(), P()),
        out_specs=(split, split, split),
        check_vma=False,
    )
```

time: 762 us -> 227 us (0.30); the launches traced: 749 us -> 226 us
  waiting for transfers between devices: 332 us -> 89.5 us
  local copies, waits for them, and re-layouts: 225 us -> 15.5 us
  matrix products: 61.7 us -> 0 us
  blocking collectives: 12.4 us -> 61.6 us
  other arithmetic: 35 us -> 0 us
  Pallas kernels: 0 us -> 23.8 us
  starting transfers between devices: 54 us -> 34.5 us
  loops' own time: 14.2 us -> 0 us
  between operations: 14.9 us -> 0.78 us
    psum x2 -> x0, waiting for transfers between devices: 223 us -> none  [the longest x1 162 us: local(): glob_pairs = lax.psum(glob_term.astype(jnp.bfloat16), 'seq')]
    all_to_all x8 -> x3, waiting for transfers between devices: 108 us -> 18.7 us  [exchange(): return lax.all_to_all(tiles, AXES, split_axis=0, concat_axis=0, tiled=True)]
    ppermute x4, waiting for transfers between devices: 0.01 us -> 70.8 us  [the longest x1 52.1 us: local(): from_prev = lax.ppermute(high, AXES, UP)]
    dot_general x12 -> x0, matrix products: 61.7 us -> none  [the longest x2 27.5 us: grad_terms(): jnp.einsum('ghtk,gthd->gkhd', dscore, queries, preferred_element_type=jnp...]
    all_to_all x1, blocking collectives: 12.4 us -> 61.6 us  [exchange(): return lax.all_to_all(tiles, AXES, split_axis=0, concat_axis=0, tiled=True)]
    scatter x2 -> x0, local copies, waits for them, and re-layouts: 40.8 us -> none  [the longest x1 33.2 us: local(): served_ids = jnp.zeros((seq_devices, capacity + 1), jnp.int32).at[senders...]
    concatenate x8 -> x0, local copies, waits for them, and re-layouts: 38.6 us -> none  [the longest x2 37.6 us: full_step(): jnp.concatenate([window_set(row_start), glob_set, rand_group], axis=1)]
    while x71 -> x0, local copies, waits for them, and re-layouts: 30.7 us -> none
  transfers between devices with their start and end apart: 14 -> 7, of which waited for: 7 -> 3; matrix products, arithmetic and copies ran while one was open for 12% -> 0% of each run, Pallas kernels for 0% -> 0%
where the time goes in v1:
time: 227 us; the launch traced here: 226 us
  waiting for transfers between devices  89.5 us (39%)
  blocking collectives  61.6 us (27%)
  starting transfers between devices  34.5 us (15%)
  Pallas kernels  23.8 us (10%)
  local copies, waits for them, and re-layouts  15.5 us (7%)
    all_to_all x1, blocking collectives, exchange(): return lax.all_to_all(tiles, AXES, split_axis=0, concat_axis=0, tiled=True)  61.6 us
    ppermute x1, waiting for transfers between devices, local(): from_prev = lax.ppermute(high, AXES, UP)  52.1 us
    all_to_all x3, starting transfers between devices, exchange(): return lax.all_to_all(tiles, AXES, split_axis=0, concat_axis=0, tiled=True)  20.9 us
    all_to_all x3, waiting for transfers between devices, exchange(): return lax.all_to_all(tiles, AXES, split_axis=0, concat_axis=0, tiled=True)  18.7 us
    ppermute x1, waiting for transfers between devices, local(): grad_from_prev = lax.ppermute(to_next, AXES, UP)  18.6 us
    unnamed x43, local copies, waits for them, and re-layouts  15.3 us
    pallas_call x1, Pallas kernels, attend(): pl.pallas_call(attend_kernel, grid_spec=pltpu.PrefetchScalarGridSpec(num_...  13.8 us
  transfers between devices with their start and end apart: 7, of which 3 were waited for; matrix products, arithmetic and copies ran while one was open for 0% of the time, Pallas kernels for 0%

profile of v1, /device:TPU:1, one launch (start us, length us, event | category | flops | bytes accessed | tf_op | source)
XLA Modules:
  0.0 225.7 jit_solution(9942660837338991444)
XLA Ops:
  0.6 0.0 copy-start.1
  0.6 1.0 copy-done.1
  1.7 0.0 copy-start.3
  1.7 1.0 copy-done.3
  2.7 1.4 pack_tiles.1
  4.1 0.0 copy-start.18
  4.1 0.8 copy-done.18
  4.9 11.5 %all-to-all-start = ((bf16[128,2,16,128]{3,2,1,0:T(8,128)(2,1)}), bf16[128,2,16,128]{3,2,1,0:T(8,128)(2,1)S(1)}, u32[]{:S(2)}, u32[]{:S(2)}) async-start(bf16[128,2,16,128]{3,2,1,0:T(8,128)(2,1)} %get-tuple-element.16), calls=%async_computation | async-start | bytes 2097152 | tf_op jit(solution)/shard_map/all_to_all | solution.py:290
  16.4 0.8 copy.9
  17.2 0.2 reshape.28.random_ref
  17.4 18.7 %all-to-all-done = bf16[128,2,16,128]{3,2,1,0:T(8,128)(2,1)S(1)} async-done(((bf16[128,2,16,128]{3,2,1,0:T(8,128)(2,1)}), bf16[128,2,16,128]{3,2,1,0:T(8,128)(2,1)S(1)}, u32[]{:S(2)}, u32[]{:S(2)}) %all-to-all-start) | async-done | bytes 1048608 | tf_op jit(solution)/shard_map/all_to_all | solution.py:290
  36.1 0.0 copy-start.16
  36.2 0.7 copy-done.16
  36.8 1.5 select_tiles.1
  38.3 0.0 copy-start
  38.3 2.0 copy-done
  40.4 0.0 copy-start.2
  40.4 0.0 copy-start.4
  40.4 0.0 copy-start.6
  40.4 0.0 copy-start.7
  40.4 4.9 %all-to-all-start.1 = ((bf16[128,8,16,128]{3,2,1,0:T(8,128)(2,1)}), bf16[128,8,16,128]{3,2,1,0:T(8,128)(2,1)}, u32[]{:S(2)}, u32[]{:S(2)}) async-start(bf16[128,8,16,128]{3,2,1,0:T(8,128)(2,1)} %copy-done), calls=%async_computation.1 | async-start | bytes 8388608 | tf_op jit(solution)/shard_map/all_to_all | solution.py:290
  45.3 3.3 %collective-permute-start = (bf16[256,1024]{1,0:T(8,128)(2,1)}, bf16[256,1024]{1,0:T(8,128)(2,1)S(1)}, u32[]{:S(2)}, u32[]{:S(2)}) collective-permute-start(bf16[256,1024]{1,0:T(8,128)(2,1)} %get-tuple-element.14), channel_id=1, source_target_pairs={{0,1},{1,2},{2,3},{3,4},{4,5},{5,6},{6,7},{7,8},{8,9},{9,10},{10,1... | collective-permute-start | bytes 1572872 | tf_op jit(solution)/shard_map/ppermute | solution.py:301
  48.7 3.5 %collective-permute-start.1 = (bf16[256,1024]{1,0:T(8,128)(2,1)}, bf16[256,1024]{1,0:T(8,128)(2,1)S(1)}, u32[]{:S(2)}, u32[]{:S(2)}) collective-permute-start(bf16[256,1024]{1,0:T(8,128)(2,1)} %copy-done.18), channel_id=1, source_target_pairs={{1,0},{2,1},{3,2},{4,3},{5,4},{6,5},{7,6},{8,7},{9,8},{10,9},{11,1... | collective-permute-start | bytes 1572872 | tf_op jit(solution)/shard_map/ppermute | solution.py:302
  52.2 52.1 %collective-permute-done.prev_ref = bf16[256,1024]{1,0:T(8,128)(2,1)S(1)} collective-permute-done((bf16[256,1024]{1,0:T(8,128)(2,1)}, bf16[256,1024]{1,0:T(8,128)(2,1)S(1)}, u32[]{:S(2)}, u32[]{:S(2)}) %collective-permute-start) | collective-permute-done | bytes 524320 | tf_op jit(solution)/shard_map/ppermute | solution.py:301
  104.3 0.0 copy-start.8
  104.3 0.8 copy-done.8
  105.1 0.0 collective-permute-done.1.next_ref
  105.1 0.0 copy-start.10
  105.1 0.8 copy-done.10
  105.9 0.0 all-to-all-done.1
  105.9 0.0 copy-done.2
  105.9 0.0 copy-done.4
  105.9 0.0 copy-done.6
  105.9 0.0 copy-done.7
  106.0 0.0 copy-start.9
  106.0 1.0 copy-done.9
  107.0 0.0 copy-start.11
  107.0 1.0 copy-done.11
  108.0 13.8 %attend.1 = (bf16[256,1024]{1,0:T(8,128)(2,1)}, f32[256,1024]{1,0:T(8,128)S(1)}, f32[256,1024]{1,0:T(8,128)}, bf16[256,1024]{1,0:T(8,128)(2,1)S(1)}, bf16[256,10...) custom-call(s32[1]{0:T(128)} %bitcast.device_ref, bf16[256,1024]{1,0:T(8,128)(2,1)S(1)} %copy-done.6, ...), custom_call_target="tpu_custom_call" | custom-call | tf_op jit(solution)/shard_map/attend/pallas_call | solution.py:206
  121.8 0.0 copy-start.19
  121.8 0.8 copy-done.19
  122.6 0.0 copy-start.20
  122.6 0.8 copy-done.20
  123.4 0.0 copy-start.17
  123.4 61.6 %all_to_all.20.terms_ref = bf16[128,8,16,128]{3,2,1,0:T(8,128)(2,1)S(1)} all-to-all(bf16[128,8,16,128]{3,2,1,0:T(8,128)(2,1)} %bitcast.8), channel_id=1, replica_groups=mesh['seq'=32,'head'=4] {'seq','head'}, dimensions={0} | all-to-all | bytes 8388608 | tf_op jit(solution)/shard_map/all_to_all | solution.py:290
  185.0 0.0 copy-done.17
  185.1 0.0 copy-start.5
  185.1 3.9 %collect_terms.1 = bf16[256,16,128]{2,1,0:T(8,128)(2,1)} custom-call(s32[768]{0:T(1024)S(1)} %reshape.28.random_ref, s32[2]{0:T(128)S(1)} %copy-done.17, bf16[128,8,16,128]{3,2,1,0:T(8,128)(2,1)S(1)} %all_to_all.20.terms_ref), custom_call_target="tpu_custom_call" | custom-call | tf_op jit(solution)/shard_map/collect_terms/pallas_call | solution.py:247
  189.0 4.5 %all-to-all-start.3 = ((bf16[128,2,16,128]{3,2,1,0:T(8,128)(2,1)}), bf16[128,2,16,128]{3,2,1,0:T(8,128)(2,1)S(1)}, u32[]{:S(2)}, u32[]{:S(2)}) async-start(bf16[128,2,16,128]{3,2,1,0:T(8,128)(2,1)} %bitcast.4), calls=%async_computation.3 | async-start | bytes 2097152 | tf_op jit(solution)/shard_map/all_to_all | solution.py:290
  193.5 3.3 %collective-permute-start.2 = (bf16[256,1024]{1,0:T(8,128)(2,1)}, bf16[256,1024]{1,0:T(8,128)(2,1)S(1)}, u32[]{:S(2)}, u32[]{:S(2)}) collective-permute-start(bf16[256,1024]{1,0:T(8,128)(2,1)} %copy-done.20), channel_id=1, source_target_pairs={{0,1},{1,2},{2,3},{3,4},{4,5},{5,6},{6,7},{7,8},{8,9},{9,10},{10,1... | collective-permute-start | bytes 1572872 | tf_op jit(solution)/shard_map/ppermute | solution.py:309
  196.8 3.5 %collective-permute-start.3 = (bf16[256,1024]{1,0:T(8,128)(2,1)}, bf16[256,1024]{1,0:T(8,128)(2,1)S(1)}, u32[]{:S(2)}, u32[]{:S(2)}) collective-permute-start(bf16[256,1024]{1,0:T(8,128)(2,1)} %copy-done.19), channel_id=1, source_target_pairs={{1,0},{2,1},{3,2},{4,3},{5,4},{6,5},{7,6},{8,7},{9,8},{10,9},{11,1... | collective-permute-start | bytes 1572872 | tf_op jit(solution)/shard_map/ppermute | solution.py:308
  200.2 18.6 %collective-permute-done.2.prev_ref = bf16[256,1024]{1,0:T(8,128)(2,1)S(1)} collective-permute-done((bf16[256,1024]{1,0:T(8,128)(2,1)}, bf16[256,1024]{1,0:T(8,128)(2,1)S(1)}, u32[]{:S(2)}, u32[]{:S(2)}) %collective-permute-start.2) | collective-permute-done | bytes 524320 | tf_op jit(solution)/shard_map/ppermute | solution.py:309
  218.9 0.0 copy-start.12
  218.9 0.8 copy-done.12
  219.7 0.0 collective-permute-done.3.next_ref
  219.7 0.0 copy-start.14
  219.7 0.8 copy-done.14
  220.5 0.0 all-to-all-done.3
  220.5 0.0 copy-done.5
  220.5 0.0 copy-start.13
  220.5 1.0 copy-done.13
  221.5 0.0 copy-start.15
  221.5 1.0 copy-done.15
  222.5 3.2 %finish.1 = (bf16[256,1024]{1,0:T(8,128)(2,1)}, bf16[256,1024]{1,0:T(8,128)(2,1)}) custom-call(f32[256,1024]{1,0:T(8,128)S(1)} %get-tuple-element.18.wk_ref, f32[256,1024]{1,0:T(8,128)S(1)} %copy-done.5, bf16[256,1024]{1,0:T(8,128)(2,1)S(1)} %copy-done.13, bf16[256,1024]{1,0:T(8,128)(2,1)S(1)} %copy-done.15, bf16[2,8,8,2,16,128]{5,4,3,2,1,0:T(8,128)(2,1)S(1)} %bitcast.6), custom_call_target="tpu_custom_call" | custom-call | tf_op jit(solution)/shard_map/finish/pallas_call | solution.py:277
Async XLA Ops:
  0.6 1.0 copy-start.1
  1.7 1.0 copy-start.3
  4.1 0.8 copy-start.18
  4.9 31.3 %all-to-all-start = ((bf16[128,2,16,128]{3,2,1,0:T(8,128)(2,1)}), bf16[128,2,16,128]{3,2,1,0:T(8,128)(2,1)S(1)}, u32[]{:S(2)}, u32[]{:S(2)}) async-start(bf16[128,2,16,128]{3,2,1,0:T(8,128)(2,1)} %get-tuple-element.16), calls=%async_computation | async-start | bytes 2097152 | tf_op jit(solution)/shard_map/all_to_all | solution.py:290
  36.1 0.7 copy-start.16
  38.3 2.0 copy-start
  40.4 65.6 %copy-start.2 = (bf16[256,1024]{1,0:T(8,128)(2,1)S(1)}, bf16[256,1024]{1,0:T(8,128)(2,1)}, u32[]{:S(2)}) copy-start(bf16[256,1024]{1,0:T(8,128)(2,1)} %k_ref.3) | copy-start | bytes 1572868
  40.4 65.6 %copy-start.4 = (bf16[256,1024]{1,0:T(8,128)(2,1)S(1)}, bf16[256,1024]{1,0:T(8,128)(2,1)}, u32[]{:S(2)}) copy-start(bf16[256,1024]{1,0:T(8,128)(2,1)} %v_ref.3) | copy-start | bytes 1572868
  40.4 65.6 %copy-start.6 = (bf16[256,1024]{1,0:T(8,128)(2,1)S(1)}, bf16[256,1024]{1,0:T(8,128)(2,1)}, u32[]{:S(2)}) copy-start(bf16[256,1024]{1,0:T(8,128)(2,1)} %q_ref.1) | copy-start | bytes 1572868
  40.4 65.6 %copy-start.7 = (bf16[256,1024]{1,0:T(8,128)(2,1)S(1)}, bf16[256,1024]{1,0:T(8,128)(2,1)}, u32[]{:S(2)}) copy-start(bf16[256,1024]{1,0:T(8,128)(2,1)} %d_ref.1) | copy-start | bytes 1572868
  40.4 65.6 %all-to-all-start.1 = ((bf16[128,8,16,128]{3,2,1,0:T(8,128)(2,1)}), bf16[128,8,16,128]{3,2,1,0:T(8,128)(2,1)}, u32[]{:S(2)}, u32[]{:S(2)}) async-start(bf16[128,8,16,128]{3,2,1,0:T(8,128)(2,1)} %copy-done), calls=%async_computation.1 | async-start | bytes 8388608 | tf_op jit(solution)/shard_map/all_to_all | solution.py:290
  45.3 59.0 %collective-permute-start = (bf16[256,1024]{1,0:T(8,128)(2,1)}, bf16[256,1024]{1,0:T(8,128)(2,1)S(1)}, u32[]{:S(2)}, u32[]{:S(2)}) collective-permute-start(bf16[256,1024]{1,0:T(8,128)(2,1)} %get-tuple-element.14), channel_id=1, source_target_pairs={{0,1},{1,2},{2,3},{3,4},{4,5},{5,6},{6,7},{7,8},{8,9},{9,10},{10,1... | collective-permute-start | bytes 1572872 | tf_op jit(solution)/shard_map/ppermute | solution.py:301
  48.7 56.5 %collective-permute-start.1 = (bf16[256,1024]{1,0:T(8,128)(2,1)}, bf16[256,1024]{1,0:T(8,128)(2,1)S(1)}, u32[]{:S(2)}, u32[]{:S(2)}) collective-permute-start(bf16[256,1024]{1,0:T(8,128)(2,1)} %copy-done.18), channel_id=1, source_target_pairs={{1,0},{2,1},{3,2},{4,3},{5,4},{6,5},{7,6},{8,7},{9,8},{10,9},{11,1... | collective-permute-start | bytes 1572872 | tf_op jit(solution)/shard_map/ppermute | solution.py:302
  104.3 0.8 copy-start.8
  105.1 0.8 copy-start.10
  106.0 1.0 copy-start.9
  107.0 1.0 copy-start.11
  121.8 0.8 copy-start.19
  122.6 0.8 copy-start.20
  123.4 61.7 %copy-start.17 = (s32[2]{0:T(128)S(1)}, s32[2]{0:T(128)}, u32[]{:S(2)}) copy-start(s32[2]{0:T(128)} %global_ref.3) | copy-start | bytes 28
  185.1 35.4 %copy-start.5 = (f32[256,1024]{1,0:T(8,128)S(1)}, f32[256,1024]{1,0:T(8,128)}, u32[]{:S(2)}) copy-start(f32[256,1024]{1,0:T(8,128)} %get-tuple-element.19.wv_ref) | copy-start | bytes 3145732
  189.0 31.5 %all-to-all-start.3 = ((bf16[128,2,16,128]{3,2,1,0:T(8,128)(2,1)}), bf16[128,2,16,128]{3,2,1,0:T(8,128)(2,1)S(1)}, u32[]{:S(2)}, u32[]{:S(2)}) async-start(bf16[128,2,16,128]{3,2,1,0:T(8,128)(2,1)} %bitcast.4), calls=%async_computation.3 | async-start | bytes 2097152 | tf_op jit(solution)/shard_map/all_to_all | solution.py:290
  193.5 25.4 %collective-permute-start.2 = (bf16[256,1024]{1,0:T(8,128)(2,1)}, bf16[256,1024]{1,0:T(8,128)(2,1)S(1)}, u32[]{:S(2)}, u32[]{:S(2)}) collective-permute-start(bf16[256,1024]{1,0:T(8,128)(2,1)} %copy-done.20), channel_id=1, source_target_pairs={{0,1},{1,2},{2,3},{3,4},{4,5},{5,6},{6,7},{7,8},{8,9},{9,10},{10,1... | collective-permute-start | bytes 1572872 | tf_op jit(solution)/shard_map/ppermute | solution.py:309
  196.8 22.9 %collective-permute-start.3 = (bf16[256,1024]{1,0:T(8,128)(2,1)}, bf16[256,1024]{1,0:T(8,128)(2,1)S(1)}, u32[]{:S(2)}, u32[]{:S(2)}) collective-permute-start(bf16[256,1024]{1,0:T(8,128)(2,1)} %copy-done.19), channel_id=1, source_target_pairs={{1,0},{2,1},{3,2},{4,3},{5,4},{6,5},{7,6},{8,7},{9,8},{10,9},{11,1... | collective-permute-start | bytes 1572872 | tf_op jit(solution)/shard_map/ppermute | solution.py:308
  218.9 0.8 copy-start.12
  219.7 0.8 copy-start.14
  220.5 1.0 copy-start.13
  221.5 1.0 copy-start.15

commit v2 on v1

v2 whole, which is shorter than its diff:
```python
import math

import jax
import jax.numpy as jnp
from jax import lax
from jax.experimental import pallas as pl
from jax.experimental.pallas import tpu as pltpu
from jax.sharding import PartitionSpec as P

HEAD_DIM = 128
BLOCK = 128
HEADS = 8
SEQ = 32
GROUPS = 4
PAIR = HEADS // GROUPS
DEVICES = SEQ * GROUPS
OWN = 2
LOCAL = OWN * GROUPS
RANDOM = 3
GLOBAL = 2
STEP = OWN * RANDOM
ASKED = LOCAL * RANDOM
ENTRIES = ASKED + GLOBAL
RETURNED = ENTRIES + 2
TILE = 16
TILES = BLOCK // TILE
BLOCKS = SEQ * LOCAL
ROWS = OWN * BLOCK
TOKENS = LOCAL * BLOCK
WIDTH = HEADS * HEAD_DIM
COLS = PAIR * HEAD_DIM
AXES = ("seq", "head")
SCALE = 1.0 / math.sqrt(HEAD_DIM)
SCALE_LOG2 = SCALE * math.log2(math.e)
MASKED = -1e30
VMEM_LIMIT = 24 * 1024 * 1024
WIDE_LIMIT = 56 * 1024 * 1024
SELECT_LIMIT = 50 * 1024 * 1024
ATTEND_LIMIT = 46 * 1024 * 1024
LOW = jnp.bfloat16


def shape_of(shape, kind=LOW):
    return jax.ShapeDtypeStruct(shape, kind)


INSIDE = pl.BlockSpec(memory_space=pltpu.VMEM)
OUTSIDE = pl.BlockSpec(memory_space=pl.ANY)


def call(kernel, name, scalars, arrays, outs, scratch=(), far_in=(), far_out=(), limit=VMEM_LIMIT):
    return pl.pallas_call(
        kernel,
        in_specs=[pl.BlockSpec(memory_space=pltpu.SMEM)] * len(scalars)
        + [OUTSIDE if i in far_in else INSIDE for i in range(len(arrays))],
        out_specs=tuple(OUTSIDE if i in far_out else INSIDE for i in range(len(outs))),
        out_shape=tuple(outs),
        scratch_shapes=list(scratch),
        compiler_params=pltpu.CompilerParams(vmem_limit_bytes=limit),
        name=name,
    )(*scalars, *arrays)


def group_columns(group):
    return pl.ds(pl.multiple_of(group * COLS, COLS), COLS)


def group_rows(group):
    return pl.ds(pl.multiple_of(group * ROWS, ROWS), ROWS)


def pack_kernel(k_ref, v_ref, tiles_ref, rows_ref, packed_ref, in_sems, out_sems):
    def fetch(part, block):
        rows = pl.ds(block * BLOCK, BLOCK)
        return pltpu.make_async_copy(
            (k_ref, v_ref)[part].at[rows, :], rows_ref.at[part, block], in_sems.at[part, block]
        )

    def ship(part, parity):
        return pltpu.make_async_copy(
            packed_ref.at[part, parity], tiles_ref.at[part, parity], out_sems.at[part, parity]
        )

    for part in range(2):
        for block in range(OWN):
            fetch(part, block).start()
    for part in range(2):
        for block in range(OWN):
            fetch(part, block).wait()
        for parity in range(PAIR):
            for group in range(GROUPS):
                for block in range(OWN):
                    packed_ref[part, parity, :, group, block] = rows_ref[
                        part, block, :, pl.ds((group * PAIR + parity) * HEAD_DIM, HEAD_DIM)
                    ].reshape(TILES, TILE, HEAD_DIM)
            ship(part, parity).start()
    for part in range(2):
        for parity in range(PAIR):
            ship(part, parity).wait()


def split_kernel(group_ref, *refs):
    for distance in range(GROUPS):
        columns = group_columns((group_ref[0] + distance) % GROUPS)
        for which in range(4):
            refs[4 + distance][which] = refs[which][:, columns]


def assemble_kernel(group_ref, *refs):
    near_ref, low_ref, high_ref = refs[GROUPS:]
    for distance in range(GROUPS):
        rows = group_rows((group_ref[0] + GROUPS - distance) % GROUPS)
        for which in range(4):
            near_ref[which, rows, :] = refs[distance][which]
    for part in range(2):
        low_ref[part] = near_ref[2 + part, :BLOCK, :]
        high_ref[part] = near_ref[2 + part, TOKENS - BLOCK :, :]


CHUNK = 4


def select_kernel(random_ref, global_ref, table_ref, out_ref, chosen_ref, sems):
    common = [table_ref[global_ref[which]] for which in range(GLOBAL)]

    def ship(chunk):
        part = pl.ds(chunk * CHUNK, CHUNK)
        return pltpu.make_async_copy(chosen_ref.at[part], out_ref.at[part], sems.at[chunk])

    def fill(chunk, carry):
        for device in range(CHUNK):
            place = chunk * CHUNK + device
            for entry in range(ASKED):
                chosen_ref[place, entry] = table_ref[random_ref[place * ASKED + entry]]
            for which in range(GLOBAL):
                chosen_ref[place, ASKED + which] = common[which]
        ship(chunk).start()
        return carry

    def drain(chunk, carry):
        ship(chunk).wait()
        return carry

    lax.fori_loop(0, SEQ // CHUNK, fill, 0)
    lax.fori_loop(0, SEQ // CHUNK, drain, 0)


def dot_nt(a, b):
    return lax.dot_general(a, b, (((1,), (1,)), ((), ())), preferred_element_type=jnp.float32)


def dot_nn(a, b):
    return lax.dot_general(a, b, (((1,), (0,)), ((), ())), preferred_element_type=jnp.float32)


def dot_tn(a, b):
    return lax.dot_general(a, b, (((0,), (0,)), ((), ())), preferred_element_type=jnp.float32)


def rows_of(block):
    return slice(block * BLOCK, (block + 1) * BLOCK)


def columns_of(head):
    return pl.ds(head * HEAD_DIM, HEAD_DIM)


def step_rows(step):
    return pl.ds(pl.multiple_of(step * ROWS, ROWS), ROWS)


def edge_block(step, head, part, own_ref, prev_ref, next_ref, block):
    columns = columns_of(head)
    if block == 0:
        index = jnp.maximum(OWN * step - 1, 0)
        absent, outer = step == 0, prev_ref
    else:
        index = jnp.minimum(OWN * step + OWN, LOCAL - 1)
        absent, outer = step == GROUPS - 1, next_ref
    rows = pl.ds(pl.multiple_of(index * BLOCK, BLOCK), BLOCK)
    return jnp.where(absent, outer[part, :, columns], own_ref[rows, columns])


def keysets(step, head, part, own_ref, prev_ref, next_ref, far_ref):
    def entry(index):
        return far_ref[part, head, :, index].reshape(BLOCK, HEAD_DIM)

    shared = jnp.concatenate(
        [own_ref[step_rows(step), columns_of(head)]]
        + [entry(ASKED + which) for which in range(GLOBAL)],
        axis=0,
    )
    private = [
        jnp.concatenate(
            [edge_block(step, head, part, own_ref, prev_ref, next_ref, block)]
            + [entry(step * STEP + block * RANDOM + r) for r in range(RANDOM)],
            axis=0,
        )
        for block in range(OWN)
    ]
    return shared, private


def to_tiles(block):
    return block.astype(LOW).reshape(TILES, TILE, HEAD_DIM)


SAVED = (GROUPS, PAIR, 6 * ROWS + BLOCK, ROWS)


def saved_parts(ref):
    return ref.at[:, :, : 4 * ROWS, :], ref.at[:, :, 4 * ROWS :, :]


def attend_kernel(
    place_ref, near_ref, prev_ref, next_ref, far_ref,
    terms_out, saved_out,
    terms_ref, saved_ref, term_sems, out_sems,
):
    place = place_ref[0]
    q_ref, d_ref, k_ref, v_ref = (near_ref.at[which] for which in range(4))
    ds_ref, low_ref = saved_parts(saved_ref)

    def ship_terms(index, start, size):
        entries = pl.ds(start, size)
        return pltpu.make_async_copy(
            terms_ref.at[:, :, :, entries], terms_out.at[:, :, :, entries], term_sems.at[index]
        )

    def ship(step):
        return [
            pltpu.make_async_copy(saved_ref.at[step], saved_out.at[step], out_sems.at[step]),
            ship_terms(step, step * STEP, STEP),
        ]

    column = lax.broadcasted_iota(jnp.int32, (1, ROWS), 1)

    def attend_head(step, head):
        queries = q_ref[step_rows(step), columns_of(head)]
        grads = d_ref[step_rows(step), columns_of(head)]
        k_shared, k_private = keysets(step, head, 0, k_ref, prev_ref, next_ref, far_ref)
        v_shared, v_private = keysets(step, head, 1, v_ref, prev_ref, next_ref, far_ref)

        s_shared = dot_nt(k_shared, queries) * SCALE_LOG2
        s_private = (
            jnp.concatenate([dot_nt(k_private[b], queries[rows_of(b)]) for b in range(OWN)], axis=1)
            * SCALE_LOG2
        )
        absent = ((column < BLOCK) & (step == 0) & (place == 0)) | (
            (column >= BLOCK) & (step == GROUPS - 1) & (place == SEQ - 1)
        )
        s_edge = jnp.where(absent, MASKED, s_private[:BLOCK])
        s_random = s_private[BLOCK:]
        p_shared = dot_nt(v_shared, grads)
        p_private = jnp.concatenate(
            [dot_nt(v_private[b], grads[rows_of(b)]) for b in range(OWN)], axis=1
        )
        row_max = jnp.maximum(
            jnp.maximum(
                jnp.max(s_shared, axis=0, keepdims=True), jnp.max(s_edge, axis=0, keepdims=True)
            ),
            jnp.max(s_random, axis=0, keepdims=True),
        )
        e_shared = jnp.exp2(s_shared - row_max)
        e_private = jnp.concatenate(
            [jnp.exp2(s_edge - row_max), jnp.exp2(s_random - row_max)], axis=0
        )
        total = jnp.sum(e_shared, axis=0, keepdims=True) + jnp.sum(
            e_private, axis=0, keepdims=True
        )
        inverse = 1.0 / total
        delta = (
            jnp.sum(e_shared * p_shared, axis=0, keepdims=True)
            + jnp.sum(e_private * p_private, axis=0, keepdims=True)
        ) * inverse

        probs_shared = e_shared * inverse
        probs_private = e_private * inverse
        low_private = probs_private.astype(LOW)
        ds_private = (probs_private * ((p_private - delta) * SCALE)).astype(LOW)
        low_ref[step, head, : 2 * ROWS, :] = probs_shared.astype(LOW)
        low_ref[step, head, 2 * ROWS :, :] = low_private[:BLOCK]
        ds_ref[step, head, : 2 * ROWS, :] = (
            probs_shared * ((p_shared - delta) * SCALE)
        ).astype(LOW)
        ds_ref[step, head, 2 * ROWS :, :] = ds_private

        for part, weights, other in ((0, ds_private, queries), (1, low_private, grads)):
            for block in range(OWN):
                terms = dot_nn(weights[BLOCK:, rows_of(block)], other[rows_of(block)])
                for r in range(RANDOM):
                    terms_ref[part, head, :, step * STEP + block * RANDOM + r] = to_tiles(
                        terms[rows_of(r)]
                    )

    for step in range(GROUPS):
        for head in range(PAIR):
            attend_head(step, head)
        for copy in ship(step):
            copy.start()
    for part, weights_ref, other_ref in ((0, ds_ref, q_ref), (1, low_ref, d_ref)):
        for head in range(PAIR):
            total = sum(
                dot_nn(
                    weights_ref[step, head, ROWS : 2 * ROWS, :],
                    other_ref[pl.ds(step * ROWS, ROWS), columns_of(head)],
                )
                for step in range(GROUPS)
            )
            for which in range(GLOBAL):
                terms_ref[part, head, :, ASKED + which] = to_tiles(total[rows_of(which)])
            for block, step in enumerate((0, GROUPS - 1)):
                terms_ref[part, head, :, ENTRIES + block] = to_tiles(
                    dot_nn(
                        weights_ref[step, head, 2 * ROWS : 2 * ROWS + BLOCK, rows_of(block)],
                        other_ref[
                            pl.ds(step * ROWS + block * BLOCK, BLOCK), columns_of(head)
                        ],
                    )
                )
    last = ship_terms(GROUPS, ASKED, RETURNED - ASKED)
    last.start()
    for step in range(GROUPS):
        for copy in ship(step):
            copy.wait()
    last.wait()


def attend(place, near, from_prev, from_next, far):
    terms_shape = (2, PAIR, TILES, RETURNED, TILE, HEAD_DIM)
    return call(
        attend_kernel,
        "attend",
        [place],
        [near, from_prev, from_next, far.reshape((2, PAIR, TILES, ENTRIES, TILE, HEAD_DIM))],
        [shape_of(terms_shape), shape_of(SAVED)],
        [
            pltpu.VMEM(terms_shape, LOW),
            pltpu.VMEM(SAVED, LOW),
            pltpu.SemaphoreType.DMA((GROUPS + 1,)),
            pltpu.SemaphoreType.DMA((GROUPS,)),
        ],
        far_out=(0, 1),
        limit=ATTEND_LIMIT,
    )


def near_kernel(
    near_ref, prev_ref, next_ref, far_ref, saved_ref, dq_ref, win_ref, sum_ref
):
    ds_ref, low_ref = saved_parts(saved_ref)
    q_ref, d_ref, k_ref = (near_ref.at[which] for which in range(3))
    sum_ref[...] = jnp.zeros_like(sum_ref)

    def near_head(step, head):
        columns = columns_of(head)
        k_shared, k_private = keysets(step, head, 0, k_ref, prev_ref, next_ref, far_ref)
        dq_shared = dot_tn(k_shared, ds_ref[step, head, : 2 * ROWS, :])
        dq_private = jnp.concatenate(
            [
                dot_tn(k_private[b], ds_ref[step, head, 2 * ROWS :, rows_of(b)])
                for b in range(OWN)
            ],
            axis=1,
        )
        dq_ref[step_rows(step), columns] = (dq_shared + dq_private).T.astype(LOW)
        start = pl.multiple_of(step * ROWS, ROWS)
        for part, weights_ref, other_ref in ((0, ds_ref, q_ref), (1, low_ref, d_ref)):
            other = other_ref[step_rows(step), columns]
            own = pl.ds(start + BLOCK, ROWS)
            sum_ref[part, own, columns] = sum_ref[part, own, columns] + dot_nn(
                weights_ref[step, head, :ROWS, :], other
            )
            for block in range(OWN):
                edge = pl.ds(start + block * (BLOCK + ROWS), BLOCK)
                sum_ref[part, edge, columns] = sum_ref[part, edge, columns] + dot_nn(
                    weights_ref[step, head, 2 * ROWS : 2 * ROWS + BLOCK, rows_of(block)],
                    other[rows_of(block)],
                )

    def body(step, carry):
        for head in range(PAIR):
            near_head(step, head)
        return carry

    lax.fori_loop(0, GROUPS, body, 0)
    for part in range(2):
        win_ref[part] = sum_ref[part, BLOCK : BLOCK + TOKENS, :]


def near_grads(near, from_prev, from_next, far, saved):
    return call(
        near_kernel,
        "near_grads",
        [],
        [
            near, from_prev, from_next,
            far.reshape((2, PAIR, TILES, ENTRIES, TILE, HEAD_DIM)), saved,
        ],
        [
            shape_of((TOKENS, COLS)),
            shape_of((2, TOKENS, COLS), jnp.float32),
        ],
        [pltpu.VMEM((2, TOKENS + 2 * BLOCK, COLS), jnp.float32)],
    )


def collect_kernel(random_ref, global_ref, terms_in, out_ref, terms_ref, sems, *sums):
    def fetch(chunk):
        part = pl.ds(chunk * CHUNK, CHUNK)
        return pltpu.make_async_copy(terms_in.at[part], terms_ref.at[part], sems.at[chunk])

    def begin(chunk, carry):
        fetch(chunk).start()
        return carry

    lax.fori_loop(0, SEQ // CHUNK, begin, 0)
    for sum_ref in sums:
        sum_ref[...] = jnp.zeros_like(sum_ref)

    def add(which, block, device, entry):
        sum_ref = sums[which % len(sums)]
        sum_ref[block] = sum_ref[block] + terms_ref[device, entry].astype(jnp.float32)

    def step(chunk, carry):
        fetch(chunk).wait()
        for inner in range(CHUNK):
            device = chunk * CHUNK + inner
            for entry in range(ASKED):
                add(entry, random_ref[device * ASKED + entry], device, entry)
            add(0, jnp.maximum(device * LOCAL - 1, 0), device, ENTRIES)
            add(1, jnp.minimum(device * LOCAL + LOCAL, BLOCKS - 1), device, ENTRIES + 1)
            carry = tuple(
                carry[which] + terms_ref[device, ASKED + which].astype(jnp.float32)
                for which in range(GLOBAL)
            )
        return carry

    zero = jnp.zeros((TILE, HEAD_DIM), jnp.float32)
    totals = lax.fori_loop(0, SEQ // CHUNK, step, (zero,) * GLOBAL)
    for which in range(GLOBAL):
        block = global_ref[which]
        sums[0][block] = sums[0][block] + totals[which]
    result = sums[0][...]
    for sum_ref in sums[1:]:
        result = result + sum_ref[...]
    out_ref[...] = result.astype(LOW)


def regroup_kernel(group_ref, dq_ref, win_ref, *outs):
    for distance, out_ref in enumerate(outs):
        rows = group_rows((group_ref[0] + distance) % GROUPS)
        out_ref[0] = dq_ref[rows, :]
        for part in range(2):
            out_ref[1 + part] = win_ref[part, rows, :].astype(LOW)


def finish_kernel(group_ref, *refs):
    far_ref, dq_ref, dk_ref, dv_ref = refs[GROUPS:]
    for distance in range(GROUPS):
        group = (group_ref[0] + GROUPS - distance) % GROUPS
        near_ref = refs[distance]
        dq_ref[:, group_columns(group)] = near_ref[0]
        for part, out_ref in enumerate((dk_ref, dv_ref)):
            for parity in range(PAIR):
                columns = pl.ds(
                    pl.multiple_of(group * COLS + parity * HEAD_DIM, HEAD_DIM), HEAD_DIM
                )
                for block in range(OWN):
                    rows = pl.ds(block * BLOCK, BLOCK)
                    far = far_ref[part, parity, :, group, block].reshape(BLOCK, HEAD_DIM)
                    near = near_ref[1 + part, rows, pl.ds(parity * HEAD_DIM, HEAD_DIM)]
                    out_ref[rows, columns] = (
                        near.astype(jnp.float32) + far.astype(jnp.float32)
                    ).astype(LOW)


def exchange(tiles, axes):
    return lax.all_to_all(tiles, axes, split_axis=0, concat_axis=0, tiled=True)


def around(parts):
    moved = [parts[0]]
    for distance in range(1, GROUPS):
        route = [(i, (i + distance) % GROUPS) for i in range(GROUPS)]
        moved.append(lax.ppermute(parts[distance], "head", route))
    return moved


def beside(up, down):
    forward = [(i, i + 1) for i in range(SEQ - 1)]
    backward = [(i + 1, i) for i in range(SEQ - 1)]
    return lax.ppermute(up, "seq", forward), lax.ppermute(down, "seq", backward)


def local(queries, keys, values, out_grad, random_blocks, global_blocks):
    place = lax.axis_index("seq").astype(jnp.int32).reshape(1)
    group = lax.axis_index("head").astype(jnp.int32).reshape(1)
    random_list = random_blocks.reshape(-1)
    tile_shape = (2, PAIR, TILES, GROUPS, OWN, TILE, HEAD_DIM)

    (tiles,) = call(
        pack_kernel,
        "pack_tiles",
        [],
        [keys, values],
        [shape_of(tile_shape)],
        [
            pltpu.VMEM((2, OWN, BLOCK, WIDTH), LOW),
            pltpu.VMEM(tile_shape, LOW),
            pltpu.SemaphoreType.DMA((2, OWN)),
            pltpu.SemaphoreType.DMA((2, PAIR)),
        ],
        far_in=(0, 1),
        far_out=(0,),
        limit=WIDE_LIMIT,
    )
    table = exchange(tiles.reshape(DEVICES, OWN, TILE, HEAD_DIM), AXES)
    split = call(
        split_kernel,
        "split_heads",
        [group],
        [queries, out_grad, keys, values],
        [shape_of((4, ROWS, COLS))] * GROUPS,
    )
    table, *split = lax.optimization_barrier((table, *split))
    edge_shape = shape_of((2, BLOCK, COLS))
    here, low, high = call(
        assemble_kernel,
        "assemble_heads",
        [group],
        around(split),
        [shape_of((4, TOKENS, COLS))] + [edge_shape] * 2,
    )
    from_prev, from_next = beside(high, low)
    (chosen,) = call(
        select_kernel,
        "select_tiles",
        [random_list, global_blocks],
        [table.reshape(BLOCKS, TILE, HEAD_DIM)],
        [shape_of((SEQ, ENTRIES, TILE, HEAD_DIM))],
        [
            pltpu.VMEM((SEQ, ENTRIES, TILE, HEAD_DIM), LOW),
            pltpu.SemaphoreType.DMA((SEQ // CHUNK,)),
        ],
        far_out=(0,),
        limit=SELECT_LIMIT,
    )
    far = exchange(chosen, "seq")
    terms, saved = attend(
        place, here, from_prev, from_next, far
    )
    returned = exchange(terms.reshape(SEQ, RETURNED, TILE, HEAD_DIM), "seq")
    dq, win = near_grads(
        here, from_prev, from_next, far, saved
    )
    back_parts = call(
        regroup_kernel,
        "regroup",
        [group],
        [dq, win],
        [shape_of((3, ROWS, COLS))] * GROUPS,
    )
    near = around(back_parts)
    returned, *near = lax.optimization_barrier((returned, *near))
    (sums,) = call(
        collect_kernel,
        "collect_terms",
        [random_list, global_blocks],
        [returned],
        [shape_of((BLOCKS, TILE, HEAD_DIM))],
        [
            pltpu.VMEM((SEQ, RETURNED, TILE, HEAD_DIM), LOW),
            pltpu.SemaphoreType.DMA((SEQ // CHUNK,)),
        ]
        + [pltpu.VMEM((BLOCKS, TILE, HEAD_DIM), jnp.float32)] * 3,
        far_in=(0,),
        limit=VMEM_LIMIT,
    )
    back = exchange(sums.reshape(DEVICES, OWN, TILE, HEAD_DIM), AXES)
    return call(
        finish_kernel,
        "finish",
        [group],
        list(near) + [back.reshape(tile_shape)],
        [shape_of((ROWS, WIDTH))] * 3,
    )


def solution(mesh):
    split = P(AXES, None)
    return jax.shard_map(
        local,
        mesh=mesh,
        in_specs=(split, split, split, split, P(), P()),
        out_specs=(split, split, split),
        check_vma=False,
    )
```

time: 227 us -> 181 us (0.80)
  blocking collectives: 61.6 us -> 27.7 us
  waiting for transfers between devices: 89.5 us -> 80 us
  local copies, waits for them, and re-layouts: 15.5 us -> 12 us
    all_to_all x1, blocking collectives: 61.6 us -> 27.7 us  [exchange(): return lax.all_to_all(tiles, axes, split_axis=0, concat_axis=0, tiled=True)]
    ppermute x4 -> x8, waiting for transfers between devices: 70.8 us -> 47.1 us  [the longest x6 40.6 us: around(): moved.append(lax.ppermute(parts[distance], 'head', route))]
    all_to_all x3, waiting for transfers between devices: 18.7 us -> 32.9 us  [exchange(): return lax.all_to_all(tiles, axes, split_axis=0, concat_axis=0, tiled=True)]
    unnamed x43 -> x31, local copies, waits for them, and re-layouts: 15.3 us -> 11.8 us
    pallas_call x5 -> x9, Pallas kernels: 23.8 us -> 24.8 us  [call(): pl.pallas_call(kernel, in_specs=[pl.BlockSpec(memory_space=pltpu.SMEM)] *...]
    ppermute x4 -> x8, starting transfers between devices: 13.6 us -> 12.9 us  [the longest x6 6.38 us: around(): moved.append(lax.ppermute(parts[distance], 'head', route))]
  transfers between devices with their start and end apart: 7 -> 11, of which waited for: 3 -> 10; matrix products, arithmetic and copies ran while one was open for 0% -> 0% of each run, Pallas kernels for 0% -> 3%
where the time goes in v2:
time: 181 us; the launch traced here: 180 us
  waiting for transfers between devices  80 us (44%)
  starting transfers between devices  35 us (19%)
  blocking collectives  27.7 us (15%)
  Pallas kernels  24.8 us (14%)
  local copies, waits for them, and re-layouts  12 us (7%)
    ppermute x6, waiting for transfers between devices, around(): moved.append(lax.ppermute(parts[distance], 'head', route))  40.6 us
    all_to_all x3, waiting for transfers between devices, exchange(): return lax.all_to_all(tiles, axes, split_axis=0, concat_axis=0, tiled=True)  32.9 us
    all_to_all x1, blocking collectives, exchange(): return lax.all_to_all(tiles, axes, split_axis=0, concat_axis=0, tiled=True)  27.7 us
    pallas_call x9, Pallas kernels, call(): pl.pallas_call(kernel, in_specs=[pl.BlockSpec(memory_space=pltpu.SMEM)] *...  24.8 us
    all_to_all x3, starting transfers between devices, exchange(): return lax.all_to_all(tiles, axes, split_axis=0, concat_axis=0, tiled=True)  22.1 us
    unnamed x31, local copies, waits for them, and re-layouts  11.8 us
    ppermute x6, starting transfers between devices, around(): moved.append(lax.ppermute(parts[distance], 'head', route))  6.38 us
    ppermute x1, starting transfers between devices, beside(): lax.ppermute(up, 'seq', forward)  4.62 us
  transfers between devices with their start and end apart: 11, of which 10 were waited for; matrix products, arithmetic and copies ran while one was open for 0% of the time, Pallas kernels for 3%

profile of v2, /device:TPU:1, one launch (start us, length us, event | category | flops | bytes accessed | tf_op | source)
XLA Modules:
  0.0 180.4 jit_solution(14299352156696565202)
XLA Ops:
  0.6 0.0 copy-start.5
  0.6 0.0 copy-start.4
  0.7 0.0 copy-start.14
  0.7 0.0 copy-start.7
  0.7 0.0 copy-start.6
  0.7 0.0 copy-start.10
  0.7 2.3 %pack_tiles.1 = bf16[2,2,8,4,2,16,128]{6,5,4,3,2,1,0:T(8,128)(2,1)} custom-call(bf16[256,1024]{1,0:T(8,128)(2,1)} %refs_2_.1, bf16[256,1024]{1,0:T(8,128)(2,1)} %refs_3_.1), custom_call_target="tpu_custom_call" | custom-call | tf_op jit(solution)/shard_map/pack_tiles/pallas_call | solution.py:52
  3.0 11.5 %all-to-all-start = ((bf16[128,2,16,128]{3,2,1,0:T(8,128)(2,1)}), bf16[128,2,16,128]{3,2,1,0:T(8,128)(2,1)S(1)}, u32[]{:S(2)}, u32[]{:S(2)}) async-start(bf16[128,2,16,128]{3,2,1,0:T(8,128)(2,1)} %bitcast.13), calls=%async_computation | async-start | bytes 2097152 | tf_op jit(solution)/shard_map/all_to_all | solution.py:479
  14.5 0.0 copy-done.14
  14.5 0.1 copy.9
  14.6 0.2 reshape.37.random_ref
  14.8 0.0 copy-done.5
  14.8 0.0 copy-done.4
  14.9 0.0 copy-done.7
  14.9 0.0 copy-done.6
  14.9 0.3 split_heads.1
  15.2 0.0 copy-start.8
  15.2 0.8 copy-done.8
  16.0 0.0 copy-start.11
  16.0 0.8 copy-done.11
  16.8 0.0 copy-start.12
  16.8 0.8 copy-done.12
  17.6 0.0 copy-start.13
  17.6 0.8 copy-done.13
  18.4 15.9 %all-to-all-done = bf16[128,2,16,128]{3,2,1,0:T(8,128)(2,1)S(1)} async-done(((bf16[128,2,16,128]{3,2,1,0:T(8,128)(2,1)}), bf16[128,2,16,128]{3,2,1,0:T(8,128)(2,1)S(1)}, u32[]{:S(2)}, u32[]{:S(2)}) %all-to-all-start) | async-done | bytes 1048608 | tf_op jit(solution)/shard_map/all_to_all | solution.py:479
  34.2 0.0 copy-done.10
  34.2 2.5 %select_tiles.1 = bf16[32,26,16,128]{3,2,1,0:T(8,128)(2,1)} custom-call(s32[768]{0:T(1024)S(1)} %reshape.37.random_ref, s32[2]{0:T(128)S(1)} %copy-done.10, bf16[256,16,128]{2,1,0:T(8,128)(2,1)S(1)} %bitcast.11), custom_call_target="tpu_custom_call" | custom-call | tf_op jit(solution)/shard_map/select_tiles/pallas_call | solution.py:52
  36.7 4.0 %all-to-all-start.1 = ((bf16[32,26,16,128]{3,2,1,0:T(8,128)(2,1)}), bf16[32,26,16,128]{3,2,1,0:T(8,128)(2,1)S(1)}, u32[]{:S(2)}, u32[]{:S(2)}) async-start(bf16[32,26,16,128]{3,2,1,0:T(8,128)(2,1)} %select_tiles.1), calls=%async_computation.1 | async-start | bytes 6815744 | tf_op jit(solution)/shard_map/all_to_all | solution.py:479
  40.7 0.4 collective-permute-start
  41.1 2.1 %collective-permute-start.1 = (bf16[4,256,256]{2,1,0:T(8,128)(2,1)}, bf16[4,256,256]{2,1,0:T(8,128)(2,1)S(1)}, u32[]{:S(2)}, u32[]{:S(2)}) collective-permute-start(bf16[4,256,256]{2,1,0:T(8,128)(2,1)} %copy-done.12), channel_id=1, source_target_pairs={{0,2},{1,3},{2,0},{3,1},{4,6},{5,7},{6,4},{7,5},{8,10},{9,11},{10,... | collective-permute-start | bytes 1572872 | tf_op jit(solution)/shard_map/ppermute | solution.py:486
  43.2 0.4 collective-permute-start.2
  43.6 12.0 %collective-permute-done.refs_1_ = bf16[4,256,256]{2,1,0:T(8,128)(2,1)S(1)} collective-permute-done((bf16[4,256,256]{2,1,0:T(8,128)(2,1)}, bf16[4,256,256]{2,1,0:T(8,128)(2,1)S(1)}, u32[]{:S(2)}, u32[]{:S(2)}) %collective-permute-start) | collective-permute-done | bytes 524320 | tf_op jit(solution)/shard_map/ppermute | solution.py:486
  55.6 10.8 %collective-permute-done.1.refs_2_ = bf16[4,256,256]{2,1,0:T(8,128)(2,1)S(1)} collective-permute-done((bf16[4,256,256]{2,1,0:T(8,128)(2,1)}, bf16[4,256,256]{2,1,0:T(8,128)(2,1)S(1)}, u32[]{:S(2)}, u32[]{:S(2)}) %collective-permute-start.1) | collective-permute-done | bytes 524320 | tf_op jit(solution)/shard_map/ppermute | solution.py:486
  66.4 0.5 collective-permute-done.2.refs_3_
  66.9 0.0 copy-start.9
  66.9 1.0 copy-done.9
  68.0 0.9 assemble_heads.1
  68.8 0.0 copy-start
  68.8 1.3 copy-done
  70.2 4.6 %collective-permute-start.3 = (bf16[2,128,256]{2,1,0:T(8,128)(2,1)}, bf16[2,128,256]{2,1,0:T(8,128)(2,1)S(1)}, u32[]{:S(2)}, u32[]{:S(2)}) collective-permute-start(bf16[2,128,256]{2,1,0:T(8,128)(2,1)} %get-tuple-element.37), channel_id=1, source_target_pairs={{0,4},{4,8},{8,12},{12,16},{16,20},{20,24},{24,28},{28,32},{32,36}... | collective-permute-start | bytes 393224 | tf_op jit(solution)/shard_map/ppermute | solution.py:493
  74.8 1.9 %collective-permute-start.4 = (bf16[2,128,256]{2,1,0:T(8,128)(2,1)}, bf16[2,128,256]{2,1,0:T(8,128)(2,1)}, u32[]{:S(2)}, u32[]{:S(2)}) collective-permute-start(bf16[2,128,256]{2,1,0:T(8,128)(2,1)} %get-tuple-element.38), channel_id=1, source_target_pairs={{4,0},{8,4},{12,8},{16,12},{20,16},{24,20},{28,24},{32,28},{36,32}... | collective-permute-start | bytes 393224 | tf_op jit(solution)/shard_map/ppermute | solution.py:493
  76.7 3.3 %collective-permute-done.3.prev_ref = bf16[2,128,256]{2,1,0:T(8,128)(2,1)S(1)} collective-permute-done((bf16[2,128,256]{2,1,0:T(8,128)(2,1)}, bf16[2,128,256]{2,1,0:T(8,128)(2,1)S(1)}, u32[]{:S(2)}, u32[]{:S(2)}) %collective-permute-start.3) | collective-permute-done | bytes 131104 | tf_op jit(solution)/shard_map/ppermute | solution.py:493
  80.0 3.2 %collective-permute-done.4.next_ref = bf16[2,128,256]{2,1,0:T(8,128)(2,1)} collective-permute-done((bf16[2,128,256]{2,1,0:T(8,128)(2,1)}, bf16[2,128,256]{2,1,0:T(8,128)(2,1)}, u32[]{:S(2)}, u32[]{:S(2)}) %collective-permute-start.4) | collective-permute-done | bytes 131104 | tf_op jit(solution)/shard_map/ppermute | solution.py:493
  83.2 0.2 all-to-all-done.1
  83.5 0.0 copy-start.1
  83.5 1.6 copy-done.1
  85.1 10.0 %attend.1 = (bf16[2,2,8,28,16,128]{5,4,3,2,1,0:T(8,128)(2,1)}, bf16[4,2,1664,256]{3,2,1,0:T(8,128)(2,1)}) custom-call(s32[1]{0:T(128)} %bitcast.1.place_ref, bf16[4,1024,256]{2,1,0:T(8,128)(2,1)S(1)} %copy-done.1, bf16[2,128,256]{2,1,0:T(8,128)(2,1)S(1)} %collective-permute-done.3.prev_ref, bf16[2,128,256]{2,1,0:T(8,128)(2,1)} %collective-permute-done.4.next_ref, ...), custom_call_target="tpu_custom_call" | custom-call | tf_op jit(solution)/shard_map/attend/pallas_call | solution.py:52
  95.0 6.6 %all-to-all-start.2 = ((bf16[32,28,16,128]{3,2,1,0:T(8,128)(2,1)}), bf16[32,28,16,128]{3,2,1,0:T(8,128)(2,1)}, u32[]{:S(2)}, u32[]{:S(2)}) async-start(bf16[32,28,16,128]{3,2,1,0:T(8,128)(2,1)} %bitcast.14), calls=%async_computation.2 | async-start | bytes 7340032 | tf_op jit(solution)/shard_map/all_to_all | solution.py:479
  101.6 0.0 copy-start.2
  101.6 1.6 copy-done.2
  103.2 0.0 copy-start.3
  103.2 2.9 %copy-done.3 = bf16[4,2,1664,256]{3,2,1,0:T(8,128)(2,1)S(1)} copy-done((bf16[4,2,1664,256]{3,2,1,0:T(8,128)(2,1)S(1)}, bf16[4,2,1664,256]{3,2,1,0:T(8,128)(2,1)}, u32[]{:S(2)}) %copy-start.3) | copy-done | bytes 6815768
  106.1 3.8 %near_grads.1 = (bf16[1024,256]{1,0:T(8,128)(2,1)S(1)}, f32[2,1024,256]{2,1,0:T(8,128)S(1)}) custom-call(bf16[4,1024,256]{2,1,0:T(8,128)(2,1)S(1)} %copy-done.2, bf16[2,128,256]{2,1,0:T(8,128)(2,1)S(1)} %collective-permute-done.3.prev_ref, bf16[2,128,256]{2,1,0:T(8,128)(2,1)} %collective-permute-done.4.next_ref, ...), custom_call_target="tpu_custom_call" | custom-call | tf_op jit(solution)/shard_map/near_grads/pallas_call | solution.py:52
  109.9 0.1 regroup.1
  110.1 0.2 collective-permute-start.5
  110.3 3.3 %collective-permute-start.6 = (bf16[3,256,256]{2,1,0:T(8,128)(2,1)S(1)}, bf16[3,256,256]{2,1,0:T(8,128)(2,1)S(1)}, u32[]{:S(2)}, u32[]{:S(2)}) collective-permute-start(bf16[3,256,256]{2,1,0:T(8,128)(2,1)S(1)} %get-tuple-element.46), channel_id=1, source_target_pairs={{0,2},{1,3},{2,0},{3,1},{4,6},{5,7},{6,4},{7,5},{8,10},{9,11},{10,... | collective-permute-start | bytes 1179656 | tf_op jit(solution)/shard_map/ppermute | solution.py:486
  113.6 0.0 collective-permute-start.7
  113.6 8.1 %collective-permute-done.5.refs_1_ = bf16[3,256,256]{2,1,0:T(8,128)(2,1)S(1)} collective-permute-done((bf16[3,256,256]{2,1,0:T(8,128)(2,1)S(1)}, bf16[3,256,256]{2,1,0:T(8,128)(2,1)S(1)}, u32[]{:S(2)}, u32[]{:S(2)}) %collective-permute-start.5) | collective-permute-done | bytes 393248 | tf_op jit(solution)/shard_map/ppermute | solution.py:486
  121.7 9.1 %collective-permute-done.6.refs_2_ = bf16[3,256,256]{2,1,0:T(8,128)(2,1)S(1)} collective-permute-done((bf16[3,256,256]{2,1,0:T(8,128)(2,1)S(1)}, bf16[3,256,256]{2,1,0:T(8,128)(2,1)S(1)}, u32[]{:S(2)}, u32[]{:S(2)}) %collective-permute-start.6) | collective-permute-done | bytes 393248 | tf_op jit(solution)/shard_map/ppermute | solution.py:486
  130.8 0.0 collective-permute-done.7.refs_3_
  130.8 16.7 %all-to-all-done.2.terms_in = bf16[32,28,16,128]{3,2,1,0:T(8,128)(2,1)} async-done(((bf16[32,28,16,128]{3,2,1,0:T(8,128)(2,1)}), bf16[32,28,16,128]{3,2,1,0:T(8,128)(2,1)}, u32[]{:S(2)}, u32[]{:S(2)}) %all-to-all-start.2) | async-done | bytes 3670048 | tf_op jit(solution)/shard_map/all_to_all | solution.py:479
  147.6 3.6 %collect_terms.1 = bf16[256,16,128]{2,1,0:T(8,128)(2,1)S(1)} custom-call(s32[768]{0:T(1024)S(1)} %reshape.37.random_ref, s32[2]{0:T(128)S(1)} %copy-done.10, bf16[32,28,16,128]{3,2,1,0:T(8,128)(2,1)} %all-to-all-done.2.terms_in), custom_call_target="tpu_custom_call" | custom-call | tf_op jit(solution)/shard_map/collect_terms/pallas_call | solution.py:52
  151.2 27.7 %all_to_all.20 = bf16[128,2,16,128]{3,2,1,0:T(8,128)(2,1)S(1)} all-to-all(bf16[128,2,16,128]{3,2,1,0:T(8,128)(2,1)S(1)} %bitcast.12), channel_id=1, replica_groups=mesh['seq'=32,'head'=4] {'seq','head'}, dimensions={0} | all-to-all | bytes 2097152 | tf_op jit(solution)/shard_map/all_to_all | solution.py:479
  178.9 1.4 finish.1
Async XLA Ops:
  0.6 14.2 %copy-start.5 = (bf16[256,1024]{1,0:T(8,128)(2,1)S(1)}, bf16[256,1024]{1,0:T(8,128)(2,1)}, u32[]{:S(2)}) copy-start(bf16[256,1024]{1,0:T(8,128)(2,1)} %refs_3_.1) | copy-start | bytes 1572868
  0.6 14.2 %copy-start.4 = (bf16[256,1024]{1,0:T(8,128)(2,1)S(1)}, bf16[256,1024]{1,0:T(8,128)(2,1)}, u32[]{:S(2)}) copy-start(bf16[256,1024]{1,0:T(8,128)(2,1)} %refs_2_.1) | copy-start | bytes 1572868
  0.7 13.8 %copy-start.14 = (s32[256,3]{0,1:T(4,128)S(1)}, s32[256,3]{0,1:T(4,128)}, u32[]{:S(2)}) copy-start(s32[256,3]{0,1:T(4,128)} %param.10) | copy-start | bytes 9220
  0.7 14.2 %copy-start.7 = (bf16[256,1024]{1,0:T(8,128)(2,1)S(1)}, bf16[256,1024]{1,0:T(8,128)(2,1)}, u32[]{:S(2)}) copy-start(bf16[256,1024]{1,0:T(8,128)(2,1)} %refs_1_.1) | copy-start | bytes 1572868
  0.7 14.2 %copy-start.6 = (bf16[256,1024]{1,0:T(8,128)(2,1)S(1)}, bf16[256,1024]{1,0:T(8,128)(2,1)}, u32[]{:S(2)}) copy-start(bf16[256,1024]{1,0:T(8,128)(2,1)} %refs_0_.1) | copy-start | bytes 1572868
  0.7 33.5 %copy-start.10 = (s32[2]{0:T(128)S(1)}, s32[2]{0:T(128)}, u32[]{:S(2)}) copy-start(s32[2]{0:T(128)} %global_ref.3) | copy-start | bytes 28
  3.0 31.3 %all-to-all-start = ((bf16[128,2,16,128]{3,2,1,0:T(8,128)(2,1)}), bf16[128,2,16,128]{3,2,1,0:T(8,128)(2,1)S(1)}, u32[]{:S(2)}, u32[]{:S(2)}) async-start(bf16[128,2,16,128]{3,2,1,0:T(8,128)(2,1)} %bitcast.13), calls=%async_computation | async-start | bytes 2097152 | tf_op jit(solution)/shard_map/all_to_all | solution.py:479
  15.2 0.8 copy-start.8
  16.0 0.8 copy-start.11
  16.8 0.8 copy-start.12
  17.6 0.8 copy-start.13
  36.7 46.8 %all-to-all-start.1 = ((bf16[32,26,16,128]{3,2,1,0:T(8,128)(2,1)}), bf16[32,26,16,128]{3,2,1,0:T(8,128)(2,1)S(1)}, u32[]{:S(2)}, u32[]{:S(2)}) async-start(bf16[32,26,16,128]{3,2,1,0:T(8,128)(2,1)} %select_tiles.1), calls=%async_computation.1 | async-start | bytes 6815744 | tf_op jit(solution)/shard_map/all_to_all | solution.py:479
  40.7 14.9 %collective-permute-start = (bf16[4,256,256]{2,1,0:T(8,128)(2,1)}, bf16[4,256,256]{2,1,0:T(8,128)(2,1)S(1)}, u32[]{:S(2)}, u32[]{:S(2)}) collective-permute-start(bf16[4,256,256]{2,1,0:T(8,128)(2,1)} %copy-done.13), channel_id=1, source_target_pairs={{0,1},{1,2},{2,3},{3,0},{4,5},{5,6},{6,7},{7,4},{8,9},{9,10},{10,1... | collective-permute-start | bytes 1572872 | tf_op jit(solution)/shard_map/ppermute | solution.py:486
  41.1 25.3 %collective-permute-start.1 = (bf16[4,256,256]{2,1,0:T(8,128)(2,1)}, bf16[4,256,256]{2,1,0:T(8,128)(2,1)S(1)}, u32[]{:S(2)}, u32[]{:S(2)}) collective-permute-start(bf16[4,256,256]{2,1,0:T(8,128)(2,1)} %copy-done.12), channel_id=1, source_target_pairs={{0,2},{1,3},{2,0},{3,1},{4,6},{5,7},{6,4},{7,5},{8,10},{9,11},{10,... | collective-permute-start | bytes 1572872 | tf_op jit(solution)/shard_map/ppermute | solution.py:486
  43.2 23.7 %collective-permute-start.2 = (bf16[4,256,256]{2,1,0:T(8,128)(2,1)}, bf16[4,256,256]{2,1,0:T(8,128)(2,1)S(1)}, u32[]{:S(2)}, u32[]{:S(2)}) collective-permute-start(bf16[4,256,256]{2,1,0:T(8,128)(2,1)} %copy-done.11), channel_id=1, source_target_pairs={{0,3},{1,0},{2,1},{3,2},{4,7},{5,4},{6,5},{7,6},{8,11},{9,8},{10,9... | collective-permute-start | bytes 1572872 | tf_op jit(solution)/shard_map/ppermute | solution.py:486
  66.9 1.0 copy-start.9
  68.8 1.3 copy-start
  70.2 9.8 %collective-permute-start.3 = (bf16[2,128,256]{2,1,0:T(8,128)(2,1)}, bf16[2,128,256]{2,1,0:T(8,128)(2,1)S(1)}, u32[]{:S(2)}, u32[]{:S(2)}) collective-permute-start(bf16[2,128,256]{2,1,0:T(8,128)(2,1)} %get-tuple-element.37), channel_id=1, source_target_pairs={{0,4},{4,8},{8,12},{12,16},{16,20},{20,24},{24,28},{28,32},{32,36}... | collective-permute-start | bytes 393224 | tf_op jit(solution)/shard_map/ppermute | solution.py:493
  74.8 8.4 %collective-permute-start.4 = (bf16[2,128,256]{2,1,0:T(8,128)(2,1)}, bf16[2,128,256]{2,1,0:T(8,128)(2,1)}, u32[]{:S(2)}, u32[]{:S(2)}) collective-permute-start(bf16[2,128,256]{2,1,0:T(8,128)(2,1)} %get-tuple-element.38), channel_id=1, source_target_pairs={{4,0},{8,4},{12,8},{16,12},{20,16},{24,20},{28,24},{32,28},{36,32}... | collective-permute-start | bytes 393224 | tf_op jit(solution)/shard_map/ppermute | solution.py:493
  83.5 1.6 copy-start.1
  95.0 52.6 %all-to-all-start.2 = ((bf16[32,28,16,128]{3,2,1,0:T(8,128)(2,1)}), bf16[32,28,16,128]{3,2,1,0:T(8,128)(2,1)}, u32[]{:S(2)}, u32[]{:S(2)}) async-start(bf16[32,28,16,128]{3,2,1,0:T(8,128)(2,1)} %bitcast.14), calls=%async_computation.2 | async-start | bytes 7340032 | tf_op jit(solution)/shard_map/all_to_all | solution.py:479
  101.6 1.6 copy-start.2
  103.2 2.9 %copy-start.3 = (bf16[4,2,1664,256]{3,2,1,0:T(8,128)(2,1)S(1)}, bf16[4,2,1664,256]{3,2,1,0:T(8,128)(2,1)}, u32[]{:S(2)}) copy-start(bf16[4,2,1664,256]{3,2,1,0:T(8,128)(2,1)} %get-tuple-element.41.saved_ref) | copy-start | bytes 20447236
  110.1 11.6 %collective-permute-start.5 = (bf16[3,256,256]{2,1,0:T(8,128)(2,1)S(1)}, bf16[3,256,256]{2,1,0:T(8,128)(2,1)S(1)}, u32[]{:S(2)}, u32[]{:S(2)}) collective-permute-start(bf16[3,256,256]{2,1,0:T(8,128)(2,1)S(1)} %get-tuple-element.45), channel_id=1, source_target_pairs={{0,1},{1,2},{2,3},{3,0},{4,5},{5,6},{6,7},{7,4},{8,9},{9,10},{10,1... | collective-permute-start | bytes 1179656 | tf_op jit(solution)/shard_map/ppermute | solution.py:486
  110.3 20.6 %collective-permute-start.6 = (bf16[3,256,256]{2,1,0:T(8,128)(2,1)S(1)}, bf16[3,256,256]{2,1,0:T(8,128)(2,1)S(1)}, u32[]{:S(2)}, u32[]{:S(2)}) collective-permute-start(bf16[3,256,256]{2,1,0:T(8,128)(2,1)S(1)} %get-tuple-element.46), channel_id=1, source_target_pairs={{0,2},{1,3},{2,0},{3,1},{4,6},{5,7},{6,4},{7,5},{8,10},{9,11},{10,... | collective-permute-start | bytes 1179656 | tf_op jit(solution)/shard_map/ppermute | solution.py:486
  113.6 17.3 %collective-permute-start.7 = (bf16[3,256,256]{2,1,0:T(8,128)(2,1)S(1)}, bf16[3,256,256]{2,1,0:T(8,128)(2,1)S(1)}, u32[]{:S(2)}, u32[]{:S(2)}) collective-permute-start(bf16[3,256,256]{2,1,0:T(8,128)(2,1)S(1)} %get-tuple-element.47), channel_id=1, source_target_pairs={{0,3},{1,0},{2,1},{3,2},{4,7},{5,4},{6,5},{7,6},{8,11},{9,8},{10,9... | collective-permute-start | bytes 1179656 | tf_op jit(solution)/shard_map/ppermute | solution.py:486

commit v3 on v2

--- a/solution.py
+++ b/solution.py
@@ -106,15 +106,53 @@
             refs[4 + distance][which] = refs[which][:, columns]
 
 
+NEAR = (4 * TOKENS + GROUPS * PAIR * TILE, COLS)
+
+
+def near_parts(near_ref):
+    return [near_ref.at[pl.ds(which * TOKENS, TOKENS), :] for which in range(4)]
+
+
+def stats_rows(step, head):
+    return pl.ds(4 * TOKENS + (step * PAIR + head) * TILE, TILE)
+
+
+def pack_rows(values):
+    row = lax.broadcasted_iota(jnp.int32, (TILE, ROWS), 0)
+    block = jnp.zeros((TILE, ROWS), jnp.float32)
+    for which, rest in enumerate(values):
+        for piece in range(3):
+            rounded = rest.astype(LOW).astype(jnp.float32)
+            block = jnp.where(row == 3 * which + piece, rounded, block)
+            rest = rest - rounded
+    return block.astype(LOW)
+
+
+def unpack_rows(block):
+    wide = block.astype(jnp.float32)
+    return [
+        (wide[i + 2 : i + 3] + wide[i + 1 : i + 2]) + wide[i : i + 1] for i in (0, 3, 6)
+    ]
+
+
 def assemble_kernel(group_ref, *refs):
     near_ref, low_ref, high_ref = refs[GROUPS:]
+    parts = near_parts(near_ref)
     for distance in range(GROUPS):
         rows = group_rows((group_ref[0] + GROUPS - distance) % GROUPS)
         for which in range(4):
-            near_ref[which, rows, :] = refs[distance][which]
+            parts[which][rows, :] = refs[distance][which]
     for part in range(2):
-        low_ref[part] = near_ref[2 + part, :BLOCK, :]
-        high_ref[part] = near_ref[2 + part, TOKENS - BLOCK :, :]
+        low_ref[part] = parts[2 + part][:BLOCK, :]
+        high_ref[part] = parts[2 + part][TOKENS - BLOCK :, :]
+    for step in range(GROUPS):
+        for head in range(PAIR):
+            scores, dprob = own_products(parts, step, head)
+            top = jnp.max(scores, axis=0, keepdims=True)
+            weight = jnp.exp2(scores - top)
+            total = jnp.sum(weight, axis=0, keepdims=True)
+            delta = jnp.sum(weight * dprob, axis=0, keepdims=True)
+            near_ref[stats_rows(step, head), :] = pack_rows([top, total, delta])
 
 
 CHUNK = 4
@@ -171,25 +209,16 @@
 
 def edge_block(step, head, part, own_ref, prev_ref, next_ref, block):
     columns = columns_of(head)
-    if block == 0:
-        index = jnp.maximum(OWN * step - 1, 0)
-        absent, outer = step == 0, prev_ref
-    else:
-        index = jnp.minimum(OWN * step + OWN, LOCAL - 1)
-        absent, outer = step == GROUPS - 1, next_ref
-    rows = pl.ds(pl.multiple_of(index * BLOCK, BLOCK), BLOCK)
-    return jnp.where(absent, outer[part, :, columns], own_ref[rows, columns])
+    if step == (0, GROUPS - 1)[block]:
+        return (prev_ref, next_ref)[block][part, :, columns]
+    return own_ref[pl.ds(step * ROWS + (-BLOCK, ROWS)[block], BLOCK), columns]
 
 
 def keysets(step, head, part, own_ref, prev_ref, next_ref, far_ref):
     def entry(index):
         return far_ref[part, head, :, index].reshape(BLOCK, HEAD_DIM)
 
-    shared = jnp.concatenate(
-        [own_ref[step_rows(step), columns_of(head)]]
-        + [entry(ASKED + which) for which in range(GLOBAL)],
-        axis=0,
-    )
+    common = jnp.concatenate([entry(ASKED + which) for which in range(GLOBAL)], axis=0)
     private = [
         jnp.concatenate(
             [edge_block(step, head, part, own_ref, prev_ref, next_ref, block)]
@@ -198,28 +227,42 @@
         )
         for block in range(OWN)
     ]
-    return shared, private
+    return common, private
 
 
 def to_tiles(block):
     return block.astype(LOW).reshape(TILES, TILE, HEAD_DIM)
 
 
-SAVED = (GROUPS, PAIR, 6 * ROWS + BLOCK, ROWS)
+SAVED = (GROUPS, PAIR, 4 * ROWS + BLOCK + TILE, ROWS)
 
 
 def saved_parts(ref):
-    return ref.at[:, :, : 4 * ROWS, :], ref.at[:, :, 4 * ROWS :, :]
+    low, final = 3 * ROWS, 4 * ROWS + BLOCK
+    return ref.at[:, :, :low, :], ref.at[:, :, low:final, :], ref.at[:, :, final:, :]
+
+
+def own_products(parts, step, head):
+    rows, columns = step_rows(step), columns_of(head)
+    queries, grads, keys, values = (part[rows, columns] for part in parts)
+    return dot_nt(keys, queries) * SCALE_LOG2, dot_nt(values, grads)
 
 
 def attend_kernel(
-    place_ref, near_ref, prev_ref, next_ref, far_ref,
+    place_ref, near_ref, prev_in, next_in, far_ref,
     terms_out, saved_out,
-    terms_ref, saved_ref, term_sems, out_sems,
+    prev_ref, next_ref, terms_ref, saved_ref, edge_sems, term_sems, out_sems,
 ):
     place = place_ref[0]
-    q_ref, d_ref, k_ref, v_ref = (near_ref.at[which] for which in range(4))
-    ds_ref, low_ref = saved_parts(saved_ref)
+    q_ref, d_ref, k_ref, v_ref = near_parts(near_ref)
+    ds_ref, low_ref, final_ref = saved_parts(saved_ref)
+
+    edge_copies = [
+        pltpu.make_async_copy(prev_in, prev_ref, edge_sems.at[0]),
+        pltpu.make_async_copy(next_in, next_ref, edge_sems.at[1]),
+    ]
+    for copy in edge_copies:
+        copy.start()
 
     def ship_terms(index, start, size):
         entries = pl.ds(start, size)
@@ -238,10 +281,11 @@
     def attend_head(step, head):
         queries = q_ref[step_rows(step), columns_of(head)]
         grads = d_ref[step_rows(step), columns_of(head)]
-        k_shared, k_private = keysets(step, head, 0, k_ref, prev_ref, next_ref, far_ref)
-        v_shared, v_private = keysets(step, head, 1, v_ref, prev_ref, next_ref, far_ref)
-
-        s_shared = dot_nt(k_shared, queries) * SCALE_LOG2
+        k_common, k_private = keysets(step, head, 0, k_ref, prev_ref, next_ref, far_ref)
+        v_common, v_private = keysets(step, head, 1, v_ref, prev_ref, next_ref, far_ref)
+        own_max, own_total, own_delta = unpack_rows(near_ref[stats_rows(step, head), :])
+
+        s_common = dot_nt(k_common, queries) * SCALE_LOG2
         s_private = (
             jnp.concatenate([dot_nt(k_private[b], queries[rows_of(b)]) for b in range(OWN)], axis=1)
             * SCALE_LOG2
@@ -251,39 +295,39 @@
         )
         s_edge = jnp.where(absent, MASKED, s_private[:BLOCK])
         s_random = s_private[BLOCK:]
-        p_shared = dot_nt(v_shared, grads)
+        p_common = dot_nt(v_common, grads)
         p_private = jnp.concatenate(
             [dot_nt(v_private[b], grads[rows_of(b)]) for b in range(OWN)], axis=1
         )
-        row_max = jnp.maximum(
-            jnp.maximum(
-                jnp.max(s_shared, axis=0, keepdims=True), jnp.max(s_edge, axis=0, keepdims=True)
-            ),
-            jnp.max(s_random, axis=0, keepdims=True),
-        )
-        e_shared = jnp.exp2(s_shared - row_max)
+        row_max = own_max
+        for scores in (s_common, s_edge, s_random):
+            row_max = jnp.maximum(row_max, jnp.max(scores, axis=0, keepdims=True))
+        e_common = jnp.exp2(s_common - row_max)
         e_private = jnp.concatenate(
             [jnp.exp2(s_edge - row_max), jnp.exp2(s_random - row_max)], axis=0
         )
-        total = jnp.sum(e_shared, axis=0, keepdims=True) + jnp.sum(
-            e_private, axis=0, keepdims=True
+        own_scale = jnp.exp2(own_max - row_max)
+        total = (
+            own_total * own_scale
+            + jnp.sum(e_common, axis=0, keepdims=True)
+            + jnp.sum(e_private, axis=0, keepdims=True)
         )
         inverse = 1.0 / total
         delta = (
-            jnp.sum(e_shared * p_shared, axis=0, keepdims=True)
+            own_delta * own_scale
+            + jnp.sum(e_common * p_common, axis=0, keepdims=True)
             + jnp.sum(e_private * p_private, axis=0, keepdims=True)
         ) * inverse
-
-        probs_shared = e_shared * inverse
+        final_ref[step, head] = pack_rows([row_max, inverse, delta])
+
+        probs_common = e_common * inverse
         probs_private = e_private * inverse
         low_private = probs_private.astype(LOW)
         ds_private = (probs_private * ((p_private - delta) * SCALE)).astype(LOW)
-        low_ref[step, head, : 2 * ROWS, :] = probs_shared.astype(LOW)
-        low_ref[step, head, 2 * ROWS :, :] = low_private[:BLOCK]
-        ds_ref[step, head, : 2 * ROWS, :] = (
-            probs_shared * ((p_shared - delta) * SCALE)
-        ).astype(LOW)
-        ds_ref[step, head, 2 * ROWS :, :] = ds_private
+        low_ref[step, head, :ROWS, :] = probs_common.astype(LOW)
+        low_ref[step, head, ROWS:, :] = low_private[:BLOCK]
+        ds_ref[step, head, :ROWS, :] = (probs_common * ((p_common - delta) * SCALE)).astype(LOW)
+        ds_ref[step, head, ROWS:, :] = ds_private
 
         for part, weights, other in ((0, ds_private, queries), (1, low_private, grads)):
             for block in range(OWN):
@@ -293,7 +337,10 @@
                         terms[rows_of(r)]
                     )
 
-    for step in range(GROUPS):
+    for step in (*range(1, GROUPS - 1), 0, GROUPS - 1):
+        if step == 0:
+            for copy in edge_copies:
+                copy.wait()
         for head in range(PAIR):
             attend_head(step, head)
         for copy in ship(step):
@@ -302,7 +349,7 @@
         for head in range(PAIR):
             total = sum(
                 dot_nn(
-                    weights_ref[step, head, ROWS : 2 * ROWS, :],
+                    weights_ref[step, head, :ROWS, :],
                     other_ref[pl.ds(step * ROWS, ROWS), columns_of(head)],
                 )
                 for step in range(GROUPS)
@@ -312,7 +359,7 @@
             for block, step in enumerate((0, GROUPS - 1)):
                 terms_ref[part, head, :, ENTRIES + block] = to_tiles(
                     dot_nn(
-                        weights_ref[step, head, 2 * ROWS : 2 * ROWS + BLOCK, rows_of(block)],
+                        weights_ref[step, head, ROWS : ROWS + BLOCK, rows_of(block)],
                         other_ref[
                             pl.ds(step * ROWS + block * BLOCK, BLOCK), columns_of(head)
                         ],
@@ -335,11 +382,15 @@
         [near, from_prev, from_next, far.reshape((2, PAIR, TILES, ENTRIES, TILE, HEAD_DIM))],
         [shape_of(terms_shape), shape_of(SAVED)],
         [
+            pltpu.VMEM((2, BLOCK, COLS), LOW),
+            pltpu.VMEM((2, BLOCK, COLS), LOW),
             pltpu.VMEM(terms_shape, LOW),
             pltpu.VMEM(SAVED, LOW),
+            pltpu.SemaphoreType.DMA((2,)),
             pltpu.SemaphoreType.DMA((GROUPS + 1,)),
             pltpu.SemaphoreType.DMA((GROUPS,)),
         ],
+        far_in=(1, 2),
         far_out=(0, 1),
         limit=ATTEND_LIMIT,
     )
@@ -348,42 +399,45 @@
 def near_kernel(
     near_ref, prev_ref, next_ref, far_ref, saved_ref, dq_ref, win_ref, sum_ref
 ):
-    ds_ref, low_ref = saved_parts(saved_ref)
-    q_ref, d_ref, k_ref = (near_ref.at[which] for which in range(3))
+    ds_ref, low_ref, final_ref = saved_parts(saved_ref)
+    parts = near_parts(near_ref)
+    q_ref, d_ref, k_ref, _ = parts
     sum_ref[...] = jnp.zeros_like(sum_ref)
 
     def near_head(step, head):
         columns = columns_of(head)
-        k_shared, k_private = keysets(step, head, 0, k_ref, prev_ref, next_ref, far_ref)
-        dq_shared = dot_tn(k_shared, ds_ref[step, head, : 2 * ROWS, :])
+        k_common, k_private = keysets(step, head, 0, k_ref, prev_ref, next_ref, far_ref)
+        row_max, inverse, delta = unpack_rows(final_ref[step, head])
+        scores, dprob = own_products(parts, step, head)
+        probs = jnp.exp2(scores - row_max) * inverse
+        own_low = probs.astype(LOW)
+        own_ds = (probs * ((dprob - delta) * SCALE)).astype(LOW)
+        dq_shared = dot_tn(k_ref[step_rows(step), columns], own_ds) + dot_tn(
+            k_common, ds_ref[step, head, :ROWS, :]
+        )
         dq_private = jnp.concatenate(
-            [
-                dot_tn(k_private[b], ds_ref[step, head, 2 * ROWS :, rows_of(b)])
-                for b in range(OWN)
-            ],
+            [dot_tn(k_private[b], ds_ref[step, head, ROWS:, rows_of(b)]) for b in range(OWN)],
             axis=1,
         )
         dq_ref[step_rows(step), columns] = (dq_shared + dq_private).T.astype(LOW)
         start = pl.multiple_of(step * ROWS, ROWS)
-        for part, weights_ref, other_ref in ((0, ds_ref, q_ref), (1, low_ref, d_ref)):
+        for part, own_weights, weights_ref, other_ref in (
+            (0, own_ds, ds_ref, q_ref),
+            (1, own_low, low_ref, d_ref),
+        ):
             other = other_ref[step_rows(step), columns]
             own = pl.ds(start + BLOCK, ROWS)
-            sum_ref[part, own, columns] = sum_ref[part, own, columns] + dot_nn(
-                weights_ref[step, head, :ROWS, :], other
-            )
+            sum_ref[part, own, columns] = sum_ref[part, own, columns] + dot_nn(own_weights, other)
             for block in range(OWN):
                 edge = pl.ds(start + block * (BLOCK + ROWS), BLOCK)
                 sum_ref[part, edge, columns] = sum_ref[part, edge, columns] + dot_nn(
-                    weights_ref[step, head, 2 * ROWS : 2 * ROWS + BLOCK, rows_of(block)],
+                    weights_ref[step, head, ROWS : ROWS + BLOCK, rows_of(block)],
                     other[rows_of(block)],
                 )
 
-    def body(step, carry):
+    for step in range(GROUPS):
         for head in range(PAIR):
             near_head(step, head)
-        return carry
-
-    lax.fori_loop(0, GROUPS, body, 0)
     for part in range(2):
         win_ref[part] = sum_ref[part, BLOCK : BLOCK + TOKENS, :]
 
@@ -456,23 +510,33 @@
 
 
 def finish_kernel(group_ref, *refs):
-    far_ref, dq_ref, dk_ref, dv_ref = refs[GROUPS:]
-    for distance in range(GROUPS):
-        group = (group_ref[0] + GROUPS - distance) % GROUPS
-        near_ref = refs[distance]
-        dq_ref[:, group_columns(group)] = near_ref[0]
-        for part, out_ref in enumerate((dk_ref, dv_ref)):
+    far_ref, *outs = refs[GROUPS : GROUPS + 4]
+    *insides, sems = refs[GROUPS + 4 :]
+
+    def ship(which):
+        return pltpu.make_async_copy(insides[which], outs[which], sems.at[which])
+
+    for which, inside in enumerate(insides):
+        for distance in range(GROUPS):
+            group = (group_ref[0] + GROUPS - distance) % GROUPS
+            near_ref = refs[distance]
+            if which == 0:
+                inside[:, group_columns(group)] = near_ref[0]
+                continue
             for parity in range(PAIR):
                 columns = pl.ds(
                     pl.multiple_of(group * COLS + parity * HEAD_DIM, HEAD_DIM), HEAD_DIM
                 )
                 for block in range(OWN):
                     rows = pl.ds(block * BLOCK, BLOCK)
-                    far = far_ref[part, parity, :, group, block].reshape(BLOCK, HEAD_DIM)
-                    near = near_ref[1 + part, rows, pl.ds(parity * HEAD_DIM, HEAD_DIM)]
-                    out_ref[rows, columns] = (
+                    far = far_ref[which - 1, parity, :, group, block].reshape(BLOCK, HEAD_DIM)
+                    near = near_ref[which, rows, columns_of(parity)]
+                    inside[rows, columns] = (
                         near.astype(jnp.float32) + far.astype(jnp.float32)
                     ).astype(LOW)
+        ship(which).start()
+    for which in range(3):
+        ship(which).wait()
 
 
 def exchange(tiles, axes):
@@ -530,7 +594,7 @@
         "assemble_heads",
         [group],
         around(split),
-        [shape_of((4, TOKENS, COLS))] + [edge_shape] * 2,
+        [shape_of(NEAR)] + [edge_shape] * 2,
     )
     from_prev, from_next = beside(high, low)
     (chosen,) = call(
@@ -584,6 +648,8 @@
         [group],
         list(near) + [back.reshape(tile_shape)],
         [shape_of((ROWS, WIDTH))] * 3,
+        [pltpu.VMEM((ROWS, WIDTH), LOW)] * 3 + [pltpu.SemaphoreType.DMA((3,))],
+        far_out=(0, 1, 2),
     )
 
 

time: 181 us -> 180 us (level)
  transfers between devices with their start and end apart: 11 -> 11, of which waited for: 10 -> 9; matrix products, arithmetic and copies ran while one was open for 0% -> 0% of each run, Pallas kernels for 3% -> 4%
where the time goes in v3:
time: 180 us; the launch traced here: 179 us
  waiting for transfers between devices  79.2 us (44%)
  starting transfers between devices  35.9 us (20%)
  blocking collectives  27.7 us (15%)
  Pallas kernels  23.8 us (13%)
  local copies, waits for them, and re-layouts  11.5 us (6%)
    ppermute x6, waiting for transfers between devices, around(): moved.append(lax.ppermute(parts[distance], 'head', route))  40.6 us
    all_to_all x3, waiting for transfers between devices, exchange(): return lax.all_to_all(tiles, axes, split_axis=0, concat_axis=0, tiled=True)  32.8 us
    all_to_all x1, blocking collectives, exchange(): return lax.all_to_all(tiles, axes, split_axis=0, concat_axis=0, tiled=True)  27.7 us
    pallas_call x9, Pallas kernels, call(): pl.pallas_call(kernel, in_specs=[pl.BlockSpec(memory_space=pltpu.SMEM)] *...  23.8 us
    all_to_all x3, starting transfers between devices, exchange(): return lax.all_to_all(tiles, axes, split_axis=0, concat_axis=0, tiled=True)  23 us
    unnamed x31, local copies, waits for them, and re-layouts  11.3 us
    ppermute x6, starting transfers between devices, around(): moved.append(lax.ppermute(parts[distance], 'head', route))  6.37 us
    ppermute x1, starting transfers between devices, beside(): lax.ppermute(up, 'seq', forward)  4.62 us
  transfers between devices with their start and end apart: 11, of which 9 were waited for; matrix products, arithmetic and copies ran while one was open for 0% of the time, Pallas kernels for 4%

profile of v3, /device:TPU:1, one launch (start us, length us, event | category | flops | bytes accessed | tf_op | source)
XLA Modules:
  0.0 179.2 jit_solution(15212192491286069032)
XLA Ops:
  0.6 0.0 copy-start.5
  0.6 0.0 copy-start.4
  0.7 0.0 copy-start.14
  0.7 0.0 copy-start.7
  0.7 0.0 copy-start.6
  0.7 0.0 copy-start.10
  0.7 2.3 %pack_tiles.1 = bf16[2,2,8,4,2,16,128]{6,5,4,3,2,1,0:T(8,128)(2,1)} custom-call(bf16[256,1024]{1,0:T(8,128)(2,1)} %refs_2_.1, bf16[256,1024]{1,0:T(8,128)(2,1)} %refs_3_.1), custom_call_target="tpu_custom_call" | custom-call | tf_op jit(solution)/shard_map/pack_tiles/pallas_call | solution.py:52
  3.0 11.5 %all-to-all-start = ((bf16[128,2,16,128]{3,2,1,0:T(8,128)(2,1)}), bf16[128,2,16,128]{3,2,1,0:T(8,128)(2,1)S(1)}, u32[]{:S(2)}, u32[]{:S(2)}) async-start(bf16[128,2,16,128]{3,2,1,0:T(8,128)(2,1)} %bitcast.13), calls=%async_computation | async-start | bytes 2097152 | tf_op jit(solution)/shard_map/all_to_all | solution.py:543
  14.5 0.0 copy-done.14
  14.5 0.1 copy.9
  14.6 0.2 reshape.37.random_ref
  14.8 0.0 copy-done.5
  14.8 0.0 copy-done.4
  14.9 0.0 copy-done.7
  14.9 0.0 copy-done.6
  14.9 0.3 split_heads.1
  15.2 0.0 copy-start.8
  15.2 0.8 copy-done.8
  16.0 0.0 copy-start.11
  16.0 0.8 copy-done.11
  16.8 0.0 copy-start.12
  16.8 0.8 copy-done.12
  17.6 0.0 copy-start.13
  17.6 0.8 copy-done.13
  18.4 15.9 %all-to-all-done = bf16[128,2,16,128]{3,2,1,0:T(8,128)(2,1)S(1)} async-done(((bf16[128,2,16,128]{3,2,1,0:T(8,128)(2,1)}), bf16[128,2,16,128]{3,2,1,0:T(8,128)(2,1)S(1)}, u32[]{:S(2)}, u32[]{:S(2)}) %all-to-all-start) | async-done | bytes 1048608 | tf_op jit(solution)/shard_map/all_to_all | solution.py:543
  34.2 0.0 copy-done.10
  34.2 2.5 %select_tiles.1 = bf16[32,26,16,128]{3,2,1,0:T(8,128)(2,1)} custom-call(s32[768]{0:T(1024)S(1)} %reshape.37.random_ref, s32[2]{0:T(128)S(1)} %copy-done.10, bf16[256,16,128]{2,1,0:T(8,128)(2,1)S(1)} %bitcast.11), custom_call_target="tpu_custom_call" | custom-call | tf_op jit(solution)/shard_map/select_tiles/pallas_call | solution.py:52
  36.7 4.0 %all-to-all-start.1 = ((bf16[32,26,16,128]{3,2,1,0:T(8,128)(2,1)}), bf16[32,26,16,128]{3,2,1,0:T(8,128)(2,1)S(1)}, u32[]{:S(2)}, u32[]{:S(2)}) async-start(bf16[32,26,16,128]{3,2,1,0:T(8,128)(2,1)} %select_tiles.1), calls=%async_computation.1 | async-start | bytes 6815744 | tf_op jit(solution)/shard_map/all_to_all | solution.py:543
  40.7 0.4 collective-permute-start
  41.1 2.1 %collective-permute-start.1 = (bf16[4,256,256]{2,1,0:T(8,128)(2,1)}, bf16[4,256,256]{2,1,0:T(8,128)(2,1)S(1)}, u32[]{:S(2)}, u32[]{:S(2)}) collective-permute-start(bf16[4,256,256]{2,1,0:T(8,128)(2,1)} %copy-done.12), channel_id=1, source_target_pairs={{0,2},{1,3},{2,0},{3,1},{4,6},{5,7},{6,4},{7,5},{8,10},{9,11},{10,... | collective-permute-start | bytes 1572872 | tf_op jit(solution)/shard_map/ppermute | solution.py:550
  43.2 0.4 collective-permute-start.2
  43.6 12.0 %collective-permute-done.refs_1_ = bf16[4,256,256]{2,1,0:T(8,128)(2,1)S(1)} collective-permute-done((bf16[4,256,256]{2,1,0:T(8,128)(2,1)}, bf16[4,256,256]{2,1,0:T(8,128)(2,1)S(1)}, u32[]{:S(2)}, u32[]{:S(2)}) %collective-permute-start) | collective-permute-done | bytes 524320 | tf_op jit(solution)/shard_map/ppermute | solution.py:550
  55.6 10.8 %collective-permute-done.1.refs_2_ = bf16[4,256,256]{2,1,0:T(8,128)(2,1)S(1)} collective-permute-done((bf16[4,256,256]{2,1,0:T(8,128)(2,1)}, bf16[4,256,256]{2,1,0:T(8,128)(2,1)S(1)}, u32[]{:S(2)}, u32[]{:S(2)}) %collective-permute-start.1) | collective-permute-done | bytes 524320 | tf_op jit(solution)/shard_map/ppermute | solution.py:550
  66.4 0.5 collective-permute-done.2.refs_3_
  66.9 0.0 copy-start.9
  66.9 1.0 copy-done.9
  68.0 1.8 assemble_heads.1
  69.7 0.0 copy-start
  69.7 1.4 copy-done
  71.1 4.6 %collective-permute-start.3 = (bf16[2,128,256]{2,1,0:T(8,128)(2,1)}, bf16[2,128,256]{2,1,0:T(8,128)(2,1)S(1)}, u32[]{:S(2)}, u32[]{:S(2)}) collective-permute-start(bf16[2,128,256]{2,1,0:T(8,128)(2,1)} %get-tuple-element.37), channel_id=1, source_target_pairs={{0,4},{4,8},{8,12},{12,16},{16,20},{20,24},{24,28},{28,32},{32,36}... | collective-permute-start | bytes 393224 | tf_op jit(solution)/shard_map/ppermute | solution.py:557
  75.7 1.9 %collective-permute-start.4 = (bf16[2,128,256]{2,1,0:T(8,128)(2,1)}, bf16[2,128,256]{2,1,0:T(8,128)(2,1)}, u32[]{:S(2)}, u32[]{:S(2)}) collective-permute-start(bf16[2,128,256]{2,1,0:T(8,128)(2,1)} %get-tuple-element.38), channel_id=1, source_target_pairs={{4,0},{8,4},{12,8},{16,12},{20,16},{24,20},{28,24},{32,28},{36,32}... | collective-permute-start | bytes 393224 | tf_op jit(solution)/shard_map/ppermute | solution.py:557
  77.6 2.4 %collective-permute-done.3.prev_in.prev_ref = bf16[2,128,256]{2,1,0:T(8,128)(2,1)S(1)} collective-permute-done((bf16[2,128,256]{2,1,0:T(8,128)(2,1)}, bf16[2,128,256]{2,1,0:T(8,128)(2,1)S(1)}, u32[]{:S(2)}, u32[]{:S(2)}) %collective-permute-start.3) | collective-permute-done | bytes 131104 | tf_op jit(solution)/shard_map/ppermute | solution.py:557
  80.0 3.4 %collective-permute-done.4.next_in.next_ref = bf16[2,128,256]{2,1,0:T(8,128)(2,1)} collective-permute-done((bf16[2,128,256]{2,1,0:T(8,128)(2,1)}, bf16[2,128,256]{2,1,0:T(8,128)(2,1)}, u32[]{:S(2)}, u32[]{:S(2)}) %collective-permute-start.4) | collective-permute-done | bytes 131104 | tf_op jit(solution)/shard_map/ppermute | solution.py:557
  83.4 0.0 all-to-all-done.1
  83.5 0.0 copy-start.1
  83.5 1.6 copy-done.1
  85.1 7.7 %attend.1 = (bf16[2,2,8,28,16,128]{5,4,3,2,1,0:T(8,128)(2,1)}, bf16[4,2,1168,256]{3,2,1,0:T(8,128)(2,1)}) custom-call(s32[1]{0:T(128)} %bitcast.1.place_ref, bf16[4224,256]{1,0:T(8,128)(2,1)S(1)} %copy-done.1, bf16[2,128,256]{2,1,0:T(8,128)(2,1)S(1)} %collective-permute-done.3.prev_in.prev_ref, bf16[2,128,256]{2,1,0:T(8,128)(2,1)} %collective-permute-done.4.next_in.next_ref, ...), custom_call_target="tpu_custom_call" | custom-call | tf_op jit(solution)/shard_map/attend/pallas_call | solution.py:52
  92.8 7.5 %all-to-all-start.2 = ((bf16[32,28,16,128]{3,2,1,0:T(8,128)(2,1)}), bf16[32,28,16,128]{3,2,1,0:T(8,128)(2,1)}, u32[]{:S(2)}, u32[]{:S(2)}) async-start(bf16[32,28,16,128]{3,2,1,0:T(8,128)(2,1)} %bitcast.14), calls=%async_computation.2 | async-start | bytes 7340032 | tf_op jit(solution)/shard_map/all_to_all | solution.py:543
  100.3 0.0 copy-start.2
  100.3 1.6 copy-done.2
  101.9 0.0 copy-start.3
  101.9 2.4 %copy-done.3 = bf16[4,2,1168,256]{3,2,1,0:T(8,128)(2,1)S(1)} copy-done((bf16[4,2,1168,256]{3,2,1,0:T(8,128)(2,1)S(1)}, bf16[4,2,1168,256]{3,2,1,0:T(8,128)(2,1)}, u32[]{:S(2)}) %copy-start.3) | copy-done | bytes 4784152
  104.3 4.2 %near_grads.1 = (bf16[1024,256]{1,0:T(8,128)(2,1)S(1)}, f32[2,1024,256]{2,1,0:T(8,128)S(1)}) custom-call(bf16[4224,256]{1,0:T(8,128)(2,1)S(1)} %copy-done.2, bf16[2,128,256]{2,1,0:T(8,128)(2,1)S(1)} %collective-permute-done.3.prev_in.prev_ref, bf16[2,128,256]{2,1,0:T(8,128)(2,1)} %collective-permute-done.4.next_in.next_ref, ...), custom_call_target="tpu_custom_call" | custom-call | tf_op jit(solution)/shard_map/near_grads/pallas_call | solution.py:52
  108.5 0.1 regroup.1
  108.7 0.2 collective-permute-start.5
  108.8 3.3 %collective-permute-start.6 = (bf16[3,256,256]{2,1,0:T(8,128)(2,1)S(1)}, bf16[3,256,256]{2,1,0:T(8,128)(2,1)S(1)}, u32[]{:S(2)}, u32[]{:S(2)}) collective-permute-start(bf16[3,256,256]{2,1,0:T(8,128)(2,1)S(1)} %get-tuple-element.46), channel_id=1, source_target_pairs={{0,2},{1,3},{2,0},{3,1},{4,6},{5,7},{6,4},{7,5},{8,10},{9,11},{10,... | collective-permute-start | bytes 1179656 | tf_op jit(solution)/shard_map/ppermute | solution.py:550
  112.1 0.0 collective-permute-start.7
  112.1 8.1 %collective-permute-done.5.refs_1_ = bf16[3,256,256]{2,1,0:T(8,128)(2,1)S(1)} collective-permute-done((bf16[3,256,256]{2,1,0:T(8,128)(2,1)S(1)}, bf16[3,256,256]{2,1,0:T(8,128)(2,1)S(1)}, u32[]{:S(2)}, u32[]{:S(2)}) %collective-permute-start.5) | collective-permute-done | bytes 393248 | tf_op jit(solution)/shard_map/ppermute | solution.py:550
  120.3 9.1 %collective-permute-done.6.refs_2_ = bf16[3,256,256]{2,1,0:T(8,128)(2,1)S(1)} collective-permute-done((bf16[3,256,256]{2,1,0:T(8,128)(2,1)S(1)}, bf16[3,256,256]{2,1,0:T(8,128)(2,1)S(1)}, u32[]{:S(2)}, u32[]{:S(2)}) %collective-permute-start.6) | collective-permute-done | bytes 393248 | tf_op jit(solution)/shard_map/ppermute | solution.py:550
  129.4 0.0 collective-permute-done.7.refs_3_
  129.4 16.9 %all-to-all-done.2.terms_in = bf16[32,28,16,128]{3,2,1,0:T(8,128)(2,1)} async-done(((bf16[32,28,16,128]{3,2,1,0:T(8,128)(2,1)}), bf16[32,28,16,128]{3,2,1,0:T(8,128)(2,1)}, u32[]{:S(2)}, u32[]{:S(2)}) %all-to-all-start.2) | async-done | bytes 3670048 | tf_op jit(solution)/shard_map/all_to_all | solution.py:543
  146.3 3.6 %collect_terms.1 = bf16[256,16,128]{2,1,0:T(8,128)(2,1)S(1)} custom-call(s32[768]{0:T(1024)S(1)} %reshape.37.random_ref, s32[2]{0:T(128)S(1)} %copy-done.10, bf16[32,28,16,128]{3,2,1,0:T(8,128)(2,1)} %all-to-all-done.2.terms_in), custom_call_target="tpu_custom_call" | custom-call | tf_op jit(solution)/shard_map/collect_terms/pallas_call | solution.py:52
  149.9 27.7 %all_to_all.20 = bf16[128,2,16,128]{3,2,1,0:T(8,128)(2,1)S(1)} all-to-all(bf16[128,2,16,128]{3,2,1,0:T(8,128)(2,1)S(1)} %bitcast.12), channel_id=1, replica_groups=mesh['seq'=32,'head'=4] {'seq','head'}, dimensions={0} | all-to-all | bytes 2097152 | tf_op jit(solution)/shard_map/all_to_all | solution.py:543
  177.6 1.4 finish.1
Async XLA Ops:
  0.6 14.2 %copy-start.5 = (bf16[256,1024]{1,0:T(8,128)(2,1)S(1)}, bf16[256,1024]{1,0:T(8,128)(2,1)}, u32[]{:S(2)}) copy-start(bf16[256,1024]{1,0:T(8,128)(2,1)} %refs_3_.1) | copy-start | bytes 1572868
  0.6 14.2 %copy-start.4 = (bf16[256,1024]{1,0:T(8,128)(2,1)S(1)}, bf16[256,1024]{1,0:T(8,128)(2,1)}, u32[]{:S(2)}) copy-start(bf16[256,1024]{1,0:T(8,128)(2,1)} %refs_2_.1) | copy-start | bytes 1572868
  0.7 13.8 %copy-start.14 = (s32[256,3]{0,1:T(4,128)S(1)}, s32[256,3]{0,1:T(4,128)}, u32[]{:S(2)}) copy-start(s32[256,3]{0,1:T(4,128)} %param.10) | copy-start | bytes 9220
  0.7 14.2 %copy-start.7 = (bf16[256,1024]{1,0:T(8,128)(2,1)S(1)}, bf16[256,1024]{1,0:T(8,128)(2,1)}, u32[]{:S(2)}) copy-start(bf16[256,1024]{1,0:T(8,128)(2,1)} %refs_1_.1) | copy-start | bytes 1572868
  0.7 14.2 %copy-start.6 = (bf16[256,1024]{1,0:T(8,128)(2,1)S(1)}, bf16[256,1024]{1,0:T(8,128)(2,1)}, u32[]{:S(2)}) copy-start(bf16[256,1024]{1,0:T(8,128)(2,1)} %refs_0_.1) | copy-start | bytes 1572868
  0.7 33.5 %copy-start.10 = (s32[2]{0:T(128)S(1)}, s32[2]{0:T(128)}, u32[]{:S(2)}) copy-start(s32[2]{0:T(128)} %global_ref.3) | copy-start | bytes 28
  3.0 31.3 %all-to-all-start = ((bf16[128,2,16,128]{3,2,1,0:T(8,128)(2,1)}), bf16[128,2,16,128]{3,2,1,0:T(8,128)(2,1)S(1)}, u32[]{:S(2)}, u32[]{:S(2)}) async-start(bf16[128,2,16,128]{3,2,1,0:T(8,128)(2,1)} %bitcast.13), calls=%async_computation | async-start | bytes 2097152 | tf_op jit(solution)/shard_map/all_to_all | solution.py:543
  15.2 0.8 copy-start.8
  16.0 0.8 copy-start.11
  16.8 0.8 copy-start.12
  17.6 0.8 copy-start.13
  36.7 46.8 %all-to-all-start.1 = ((bf16[32,26,16,128]{3,2,1,0:T(8,128)(2,1)}), bf16[32,26,16,128]{3,2,1,0:T(8,128)(2,1)S(1)}, u32[]{:S(2)}, u32[]{:S(2)}) async-start(bf16[32,26,16,128]{3,2,1,0:T(8,128)(2,1)} %select_tiles.1), calls=%async_computation.1 | async-start | bytes 6815744 | tf_op jit(solution)/shard_map/all_to_all | solution.py:543
  40.7 14.9 %collective-permute-start = (bf16[4,256,256]{2,1,0:T(8,128)(2,1)}, bf16[4,256,256]{2,1,0:T(8,128)(2,1)S(1)}, u32[]{:S(2)}, u32[]{:S(2)}) collective-permute-start(bf16[4,256,256]{2,1,0:T(8,128)(2,1)} %copy-done.13), channel_id=1, source_target_pairs={{0,1},{1,2},{2,3},{3,0},{4,5},{5,6},{6,7},{7,4},{8,9},{9,10},{10,1... | collective-permute-start | bytes 1572872 | tf_op jit(solution)/shard_map/ppermute | solution.py:550
  41.1 25.3 %collective-permute-start.1 = (bf16[4,256,256]{2,1,0:T(8,128)(2,1)}, bf16[4,256,256]{2,1,0:T(8,128)(2,1)S(1)}, u32[]{:S(2)}, u32[]{:S(2)}) collective-permute-start(bf16[4,256,256]{2,1,0:T(8,128)(2,1)} %copy-done.12), channel_id=1, source_target_pairs={{0,2},{1,3},{2,0},{3,1},{4,6},{5,7},{6,4},{7,5},{8,10},{9,11},{10,... | collective-permute-start | bytes 1572872 | tf_op jit(solution)/shard_map/ppermute | solution.py:550
  43.2 23.7 %collective-permute-start.2 = (bf16[4,256,256]{2,1,0:T(8,128)(2,1)}, bf16[4,256,256]{2,1,0:T(8,128)(2,1)S(1)}, u32[]{:S(2)}, u32[]{:S(2)}) collective-permute-start(bf16[4,256,256]{2,1,0:T(8,128)(2,1)} %copy-done.11), channel_id=1, source_target_pairs={{0,3},{1,0},{2,1},{3,2},{4,7},{5,4},{6,5},{7,6},{8,11},{9,8},{10,9... | collective-permute-start | bytes 1572872 | tf_op jit(solution)/shard_map/ppermute | solution.py:550
  66.9 1.0 copy-start.9
  69.7 1.4 copy-start
  71.1 8.9 %collective-permute-start.3 = (bf16[2,128,256]{2,1,0:T(8,128)(2,1)}, bf16[2,128,256]{2,1,0:T(8,128)(2,1)S(1)}, u32[]{:S(2)}, u32[]{:S(2)}) collective-permute-start(bf16[2,128,256]{2,1,0:T(8,128)(2,1)} %get-tuple-element.37), channel_id=1, source_target_pairs={{0,4},{4,8},{8,12},{12,16},{16,20},{20,24},{24,28},{28,32},{32,36}... | collective-permute-start | bytes 393224 | tf_op jit(solution)/shard_map/ppermute | solution.py:557
  75.7 7.7 %collective-permute-start.4 = (bf16[2,128,256]{2,1,0:T(8,128)(2,1)}, bf16[2,128,256]{2,1,0:T(8,128)(2,1)}, u32[]{:S(2)}, u32[]{:S(2)}) collective-permute-start(bf16[2,128,256]{2,1,0:T(8,128)(2,1)} %get-tuple-element.38), channel_id=1, source_target_pairs={{4,0},{8,4},{12,8},{16,12},{20,16},{24,20},{28,24},{32,28},{36,32}... | collective-permute-start | bytes 393224 | tf_op jit(solution)/shard_map/ppermute | solution.py:557
  83.5 1.6 copy-start.1
  92.8 53.5 %all-to-all-start.2 = ((bf16[32,28,16,128]{3,2,1,0:T(8,128)(2,1)}), bf16[32,28,16,128]{3,2,1,0:T(8,128)(2,1)}, u32[]{:S(2)}, u32[]{:S(2)}) async-start(bf16[32,28,16,128]{3,2,1,0:T(8,128)(2,1)} %bitcast.14), calls=%async_computation.2 | async-start | bytes 7340032 | tf_op jit(solution)/shard_map/all_to_all | solution.py:543
  100.3 1.6 copy-start.2
  101.9 2.4 %copy-start.3 = (bf16[4,2,1168,256]{3,2,1,0:T(8,128)(2,1)S(1)}, bf16[4,2,1168,256]{3,2,1,0:T(8,128)(2,1)}, u32[]{:S(2)}) copy-start(bf16[4,2,1168,256]{3,2,1,0:T(8,128)(2,1)} %get-tuple-element.41.saved_ref) | copy-start | bytes 14352388
  108.7 11.6 %collective-permute-start.5 = (bf16[3,256,256]{2,1,0:T(8,128)(2,1)S(1)}, bf16[3,256,256]{2,1,0:T(8,128)(2,1)S(1)}, u32[]{:S(2)}, u32[]{:S(2)}) collective-permute-start(bf16[3,256,256]{2,1,0:T(8,128)(2,1)S(1)} %get-tuple-element.45), channel_id=1, source_target_pairs={{0,1},{1,2},{2,3},{3,0},{4,5},{5,6},{6,7},{7,4},{8,9},{9,10},{10,1... | collective-permute-start | bytes 1179656 | tf_op jit(solution)/shard_map/ppermute | solution.py:550
  108.8 20.6 %collective-permute-start.6 = (bf16[3,256,256]{2,1,0:T(8,128)(2,1)S(1)}, bf16[3,256,256]{2,1,0:T(8,128)(2,1)S(1)}, u32[]{:S(2)}, u32[]{:S(2)}) collective-permute-start(bf16[3,256,256]{2,1,0:T(8,128)(2,1)S(1)} %get-tuple-element.46), channel_id=1, source_target_pairs={{0,2},{1,3},{2,0},{3,1},{4,6},{5,7},{6,4},{7,5},{8,10},{9,11},{10,... | collective-permute-start | bytes 1179656 | tf_op jit(solution)/shard_map/ppermute | solution.py:550
  112.1 17.3 %collective-permute-start.7 = (bf16[3,256,256]{2,1,0:T(8,128)(2,1)S(1)}, bf16[3,256,256]{2,1,0:T(8,128)(2,1)S(1)}, u32[]{:S(2)}, u32[]{:S(2)}) collective-permute-start(bf16[3,256,256]{2,1,0:T(8,128)(2,1)S(1)} %get-tuple-element.47), channel_id=1, source_target_pairs={{0,3},{1,0},{2,1},{3,2},{4,7},{5,4},{6,5},{7,6},{8,11},{9,8},{10,9... | collective-permute-start | bytes 1179656 | tf_op jit(solution)/shard_map/ppermute | solution.py:550
